TPU v7x, 256 devices: a whole 4x4x8 slice. The times are simulated.
256 devices in a mesh: group: 2 (over x_lo), batch: 4 (over x_hi, core), mp: 32 (over z, y).
Axes of the slice: x: 4 (x_hi: 2, x_lo: 2; x = x_hi * 2 + x_lo), y: 4, z: 8, core: 2. Of those that a mesh axis runs over, the one named last changes fastest.
Arguments:
- pol_hidden: bfloat16 [128, 8192], P('batch'), may hold values from -6 to 6
- pol_gain: float32 [8192], replicated, may hold values from 0.1 to 1.9
- pol_head: bfloat16 [8192, 65536], P(None, ('group', 'batch', 'mp')), may hold values from -16 to 16
- cand_ids: int32 [128, 10], replicated, may hold values from 0 to 65535
- ext_hidden: bfloat16 [640, 8192], P('batch'), may hold values from -6 to 6
- ext_gain: float32 [8192], replicated, may hold values from 0.1 to 1.9
- query_w: bfloat16 [8192, 8192], P('batch', ('group', 'mp')), may hold values from -10 to 10
- key_w: bfloat16 [8192, 8192], P('batch', ('group', 'mp')), may hold values from -0.0625 to 0.0625
- value_w: bfloat16 [8192, 8192], P('batch', ('group', 'mp')), may hold values from -0.0625 to 0.0625
- key_cache: bfloat16 [64, 256, 8192], P('batch', None, ('group', 'mp')), may hold values from -10 to 10
- value_cache: bfloat16 [64, 256, 8192], P('batch', None, ('group', 'mp')), may hold values from -6 to 6
- cache_len: int32 [64], P('batch'), may hold values from 64 to 256, as said below
- score_head: float32 [8192], P(('group', 'mp')), may hold values from -4 to 4
- prev_logprob: float32 [64, 10], P('batch'), may hold values from -12 to -0.5
Outputs:
- cand_logprob: float32 [128, 10], P('batch')
- combined: float32 [64, 10], P('batch')
Inputs may be any that keep to these rules, and one draw needn't show every extreme that they name: `cache_len`: every prefix has at least 64 valid positions; some prefix has all 256.
All inputs are finite; a program needn't handle non-finite values.
Results may differ from a plain program's by a relative error of at most 0.006.
Values may be sent and summed in bfloat16 or wider, within the bound.
A program may use at most 128 MiB of HBM per device.

v0:
```python
import jax
import jax.numpy as jnp
from jax import lax
from jax.sharding import PartitionSpec as P


def rms_norm(hidden, gain):
    values = hidden.astype(jnp.float32)
    spread = jnp.mean(values * values, axis=-1, keepdims=True)
    return (values * lax.rsqrt(spread + 1e-05) * gain).astype(jnp.bfloat16)


def on_device(
    pol_hidden,
    pol_gain,
    pol_head,
    cand_ids,
    ext_hidden,
    ext_gain,
    query_w,
    key_w,
    value_w,
    key_cache,
    value_cache,
    cache_len,
    score_head,
    prev_logprob,
):
    pol_normed = rms_norm(pol_hidden, pol_gain)
    width = pol_head.shape[1]
    first_col = lax.axis_index(("group", "batch", "mp")) * width
    logits = jnp.dot(
        lax.all_gather(pol_normed, "batch", axis=0, tiled=True),
        pol_head,
        preferred_element_type=jnp.float32,
    )
    offsets = cand_ids - first_col
    columns = jnp.arange(width, dtype=jnp.int32)
    onehot = offsets[:, :, None] == columns[None, None, :]
    picked = jnp.sum(jnp.where(onehot, logits[:, None, :], 0.0), axis=-1)
    local_peak = jnp.max(logits, axis=1)
    top = lax.pmax(local_peak, ("group", "batch", "mp"))
    local_total = jnp.sum(jnp.exp(logits - top[:, None]), axis=1)
    total, cand_logit = lax.psum((local_total, picked), ("group", "batch", "mp"))
    logprob = cand_logit - top[:, None] - jnp.log(total)[:, None]
    own_rows = pol_hidden.shape[0]
    cand_logprob = lax.dynamic_slice_in_dim(
        logprob, lax.axis_index("batch") * own_rows, own_rows, 0
    )
    ext_normed = rms_norm(ext_hidden, ext_gain)
    ext_rows = ext_hidden.shape[0]
    head_width = query_w.shape[1]
    pieces = (
        lax.all_gather(query_w, "batch", axis=0, tiled=True),
        lax.all_gather(key_w, "batch", axis=0, tiled=True),
        lax.all_gather(value_w, "batch", axis=0, tiled=True),
    )
    query, key_new, value_new = tuple(
        (
            jnp.dot(ext_normed, weight_part, preferred_element_type=jnp.float32)
            for weight_part in pieces
        )
    )
    prefixes = key_cache.shape[0]
    context = key_cache.shape[1]
    cands = ext_rows // prefixes
    query = query.astype(jnp.bfloat16).reshape(prefixes, cands, head_width)
    key_new = key_new.astype(jnp.bfloat16).reshape(prefixes, cands, head_width)
    value_new = value_new.astype(jnp.bfloat16).reshape(prefixes, cands, head_width)
    scale = 1.0 / head_width**0.5
    scores = (
        jnp.einsum("pcd,ptd->pct", query, key_cache, preferred_element_type=jnp.float32) * scale
    )
    valid = (jnp.arange(context, dtype=jnp.int32)[None, :] < cache_len[:, None])[:, None, :]
    scores = jnp.where(valid, scores, -1e30)
    own = jnp.sum(query.astype(jnp.float32) * key_new.astype(jnp.float32), axis=-1) * scale
    peak = jnp.maximum(jnp.max(scores, axis=-1), own)
    expo = jnp.where(valid, jnp.exp(scores - peak[..., None]), 0.0)
    own_expo = jnp.exp(own - peak)
    whole = jnp.sum(expo, axis=-1) + own_expo
    weights = (expo / whole[..., None]).astype(jnp.bfloat16)
    own_weight = (own_expo / whole).astype(jnp.bfloat16).astype(jnp.float32)
    attended = jnp.einsum("pct,ptd->pcd", weights, value_cache, preferred_element_type=jnp.float32)
    attended = attended + own_weight[..., None] * value_new.astype(jnp.float32)
    partial_value = jnp.sum(attended * score_head[None, None, :], axis=-1)
    reward = lax.psum(partial_value, ("group", "mp"))
    combined = reward + prev_logprob
    return (cand_logprob, combined)


def solution(mesh):
    placed = (
        P("batch", None),
        P(),
        P(None, ("group", "batch", "mp")),
        P(),
        P("batch", None),
        P(),
        P("batch", ("group", "mp")),
        P("batch", ("group", "mp")),
        P("batch", ("group", "mp")),
        P("batch", None, ("group", "mp")),
        P("batch", None, ("group", "mp")),
        P("batch"),
        P(("group", "mp")),
        P("batch", None),
    )
    return jax.shard_map(
        on_device,
        mesh=mesh,
        in_specs=placed,
        out_specs=(P("batch", None), P("batch", None)),
        check_vma=False,
    )
```

profile of v0, /device:TPU:2, one launch (start us, length us, event | category | flops | bytes accessed | tf_op | source)
XLA Modules:
  0.0 391.5 jit_solution(3642732124046009505)
XLA Ops:
  7.2 0.0 copy-start
  7.2 0.0 all-gather.5.cloned.1.call-start
  7.2 1.3 fusion.10
  8.6 2.1 fusion.12
  10.7 0.0 copy-start.3
  10.7 0.0 copy-start.2
  10.7 0.0 all-gather.5.cloned.1.call-update
  10.7 0.0 all-gather.7.cloned.1.call-start
  10.7 0.7 all-gather.7.cloned.1.call-update
  11.4 0.0 all-gather.11.cloned.1.call-start
  11.5 0.7 all-gather.11.cloned.1.call-update
  12.2 0.0 all-gather.9.cloned.1.call-start
  12.2 0.5 all-gather.9.cloned.1.call-update
  12.8 2.4 fusion
  15.1 0.0 copy-done.3
  15.1 0.1 iota_compare_fusion.1
  15.2 0.0 copy-done.2
  15.2 0.0 copy-start.5
  15.2 26.8 %all-gather.5.cloned.1.call-done = bf16[128,8192]{1,0:T(8,128)(2,1)} async-done(((bf16[32,8192]{1,0:T(8,128)(2,1)}), bf16[128,8192]{1,0:T(8,128)(2,1)}) %all-gather.5.cloned.1.call-update) | async-done | bytes 2097168 | tf_op jit(solution)/shard_map/all_gather | solution.py:33
  42.1 3.6 fusion.25
  45.7 92.0 %pmax.7 = f32[128]{0:T(128)S(1)} all-reduce(f32[128]{0:T(128)S(1)} %get-tuple-element.6), channel_id=1, replica_groups=mesh['group'=2,'batch'=4,'mp'=32] {'group','batch','mp'}, use_global_device_ids=true, to_apply=%region_4.5 | all-reduce | flops 128 | bytes 1024 | tf_op jit(solution)/shard_map/pmax | solution.py:42
  137.7 0.2 exponential_reduce_fusion
  137.8 0.5 select_reduce_fusion
  138.3 75.0 %all-reduce = (f32[128,10]{0,1:T(8,128)S(1)}, f32[128]{0:T(128)S(1)}) all-reduce(f32[128,10]{0,1:T(8,128)S(1)} %select_reduce_fusion, f32[128]{0:T(128)S(1)} %exponential_reduce_fusion), channel_id=1, replica_groups=mesh['group'=2,'batch'=4,'mp'=32] {'group','batch','mp'}, use_global_device_ids=true, to_apply=%region_2.3 | all-reduce | flops 1408 | bytes 11264 | tf_op jit(solution)/shard_map/psum | solution.py:44
  213.3 0.1 dynamic-slice
  213.3 0.1 dynamic-slice.1
  213.4 0.0 all-gather.7.cloned.1.call-done
  213.4 0.0 copy-done.5
  213.4 3.4 convolution_convert_fusion.2
  216.8 0.0 all-gather.11.cloned.1.call-done
  216.8 3.4 fusion.6
  220.2 0.0 copy-start.4
  220.3 0.0 copy-start.6
  220.3 0.0 all-gather.9.cloned.1.call-done
  220.3 3.5 fusion.9
  223.8 0.0 copy-start.1
  223.9 0.1 mul.111
  223.9 0.0 copy-done
  224.0 0.5 fusion.26
  224.4 0.2 fusion.13
  224.7 0.0 copy-done.4
  224.7 0.0 copy-done.6
  224.7 0.4 fusion.5
  225.1 158.6 %psum.23 = f32[16,10]{1,0:T(8,128)S(1)} all-reduce(f32[16,10]{1,0:T(8,128)S(1)} %fusion.5), channel_id=1, replica_groups=mesh['group'=2,'batch'=4,'mp'=32] {'group','mp'}, use_global_device_ids=true, to_apply=%region_12.13 | all-reduce | flops 160 | bytes 1280 | tf_op jit(solution)/shard_map/psum | solution.py:86
  383.7 0.0 copy-done.1
  383.7 0.6 add.62
  384.3 0.7 fusion.18
  (9 shorter events, 0.1 us)
Async XLA Ops:
  7.2 216.8 %copy-start = (bf16[16,256,128]{2,1,0:T(8,128)(2,1)S(1)}, bf16[16,256,128]{2,1,0:T(8,128)(2,1)}, u32[]{:S(2)}) copy-start(bf16[16,256,128]{2,1,0:T(8,128)(2,1)} %param.23) | copy-start | bytes 3145732
  7.2 34.9 %all-gather.5.cloned.1.call-start = ((), (), s32[]{:S(2)}) async-start(), calls=%async_computation | async-start | bytes 2621440 | tf_op jit(solution)/shard_map/all_gather | solution.py:33
  10.7 4.5 %copy-start.3 = (s32[16]{0:T(128)S(1)}, s32[16]{0:T(128)}, u32[]{:S(2)}) copy-start(s32[16]{0:T(128)} %param.25) | copy-start | bytes 196
  10.7 4.5 %copy-start.2 = (s32[128,10]{0,1:T(8,128)S(1)}, s32[128,10]{0,1:T(8,128)}, u32[]{:S(2)}) copy-start(s32[128,10]{0,1:T(8,128)} %param.17) | copy-start | bytes 15364
  10.7 202.7 %all-gather.7.cloned.1.call-start = ((), (), s32[]{:S(2)}) async-start(), calls=%async_computation.1 | async-start | bytes 2621440 | tf_op jit(solution)/shard_map/all_gather | solution.py:54
  11.4 205.4 %all-gather.11.cloned.1.call-start = ((), (), s32[]{:S(2)}) async-start(), calls=%async_computation.3 | async-start | bytes 2621440 | tf_op jit(solution)/shard_map/all_gather | solution.py:56
  12.2 208.1 %all-gather.9.cloned.1.call-start = ((), (), s32[]{:S(2)}) async-start(), calls=%async_computation.2 | async-start | bytes 2621440 | tf_op jit(solution)/shard_map/all_gather | solution.py:55
  15.2 198.2 %copy-start.5 = (f32[8192]{0:T(1024)S(1)}, f32[8192]{0:T(1024)}, u32[]{:S(2)}) copy-start(f32[8192]{0:T(1024)} %param.19) | copy-start | bytes 98308
  220.2 4.4 %copy-start.4 = (bf16[16,256,128]{2,1,0:T(8,128)(2,1)S(1)}, bf16[16,256,128]{2,1,0:T(8,128)(2,1)}, u32[]{:S(2)}) copy-start(bf16[16,256,128]{2,1,0:T(8,128)(2,1)} %param.24) | copy-start | bytes 3145732
  220.3 4.4 %copy-start.6 = (f32[128]{0:T(128)S(1)}, f32[128]{0:T(128)}, u32[]{:S(2)}) copy-start(f32[128]{0:T(128)} %param.26) | copy-start | bytes 1540
  223.8 159.9 %copy-start.1 = (f32[16,10]{1,0:T(8,128)S(1)}, f32[16,10]{1,0:T(8,128)}, u32[]{:S(2)}) copy-start(f32[16,10]{1,0:T(8,128)} %param.27) | copy-start | bytes 1924
Sparse Core Ops, SparseCore 0:
  10.8 31.2 all-gather.4
  43.9 28.8 all-gather.6
  74.6 28.5 all-gather.10
  104.8 29.1 all-gather.8
where the time goes:
time: 392 us
  blocking collectives  326 us (83%)
  waiting for transfers between devices  28.8 us (7%)
  matrix products  14.7 us (4%)
  between operations  13.9 us (4%)
  other arithmetic  8.02 us (2%)
    psum x1, blocking collectives, on_device(): reward = lax.psum(partial_value, ('group', 'mp'))  159 us
    pmax x1, blocking collectives, on_device(): top = lax.pmax(local_peak, ('group', 'batch', 'mp'))  92 us
    psum x1, blocking collectives, on_device(): lax.psum((local_total, picked), ('group', 'batch', 'mp'))  75 us
    all_gather x1, waiting for transfers between devices, on_device(): lax.all_gather(pol_normed, 'batch', axis=0, tiled=True)  26.8 us
    dot_general x3, matrix products, on_device(): jnp.dot(ext_normed, weight_part, preferred_element_type=jnp.float32)  10.3 us
  transfers between devices with their start and end apart: 4, of which 1 were waited for; matrix products, arithmetic and copies ran while one was open for 3% of the time, Pallas kernels for 0%

commit v1 on v0

v1 whole, which is shorter than its diff:
```python
import functools

import jax
import jax.numpy as jnp
from jax import lax
from jax.experimental import pallas as pl
from jax.experimental.pallas import tpu as pltpu
from jax.sharding import PartitionSpec as P

MESH = pl.DeviceIdType.MESH
F32 = jnp.float32
BF16 = jnp.bfloat16

D = 8192
HD = 128
CAND = 10
CTX = 256
EROWS = 160
HALF = 80
PROWS = 32
SLICE = 2048
CH = 512
VOC = 256


def kernel(
    ph, pg, phead, ids, eh, eg, qw, kw, vw, kc, vc, clen, sh, prev,
    lp_out, rw_out,
    H, EG, PH, PG, PW, IDS, W, KC, VC, CL, SH, PV,
    XR, SB, OB, XP, ACC, SO, RO, ST, RT, CS, CR, R1, R2, R3,
    lsem, ssem, r_pull, r_sib, r_y, r_z, r_psib, r_pp, r_pn, r_pf, r_so, r_st, r_cr, r_1, r_2, r_3,
):
    g = lax.axis_index("group")
    b = lax.axis_index("batch")
    m = lax.axis_index("mp")
    y, z, h, c = m % 4, m // 4, b // 2, b % 2
    oh = 1 - h

    def dev(dg, dh, y_, z_, c_):
        return (dg, 2 * dh + c_, 4 * z_ + y_)

    sib = dev(g, h, y, z, 1 - c)
    opp = [dev(1 - g, oh, y, z, k) for k in range(2)]
    xp_same = dev(g, oh, y, z, c)
    xp_other = dev(g, oh, y, z, 1 - c)
    ydev = [dev(g, h, (y + k) % 4, z, c) for k in range(4)]
    gydev = [dev(1 - g, h, (y + k) % 4, z, c) for k in range(4)]
    zdev = [dev(g, h, y, (z + k) % 8, c) for k in range(8)]

    def load(src, dst, k):
        cp = pltpu.make_async_copy(src, dst, lsem.at[k])
        cp.start()
        return cp

    l_h = [load(eh.at[pl.ds(HALF * s, HALF)], H.at[pl.ds(HALF * s, HALF)], s) for s in range(2)]
    l_eg = load(eg, EG, 2)

    everyone = [sib, *opp, xp_same, xp_other, *ydev[1:], *gydev, *zdev[1:]]
    barrier = pltpu.get_barrier_semaphore()
    for other in everyone:
        pl.semaphore_signal(barrier, inc=1, device_id=other, device_id_type=MESH)

    sends = []

    def send(src, dst, rsem, target):
        cp = pltpu.make_async_remote_copy(
            src_ref=src, dst_ref=dst, send_sem=ssem.at[len(sends)], recv_sem=rsem,
            device_id=target, device_id_type=MESH,
        )
        cp.start()
        sends.append(cp)

    def got(region, rsem):
        pltpu.make_async_copy(region, region, rsem).wait()

    def row_scale(ref, rows):
        acc = jnp.zeros((16, 512), F32)
        for k in range(D // 512):
            v = ref[rows, pl.ds(512 * k, 512)].astype(F32)
            acc = acc + v * v
        mean = jnp.sum(acc, axis=1, keepdims=True) * (1.0 / D)
        return lax.rsqrt(mean + 1e-05)

    jj = y * (1 - c) + (z % 4) * c

    def norm_piece(ref, gain, rows, r, start, width):
        cols = pl.ds(pl.multiple_of(start, 128), width)
        return (ref[rows, cols].astype(F32) * r * gain[:, cols]).astype(BF16)

    def ext_norm(i, _):
        rows = pl.ds(pl.multiple_of(16 * i, 16), 16)
        r = row_scale(H, rows)
        for k in range(2):
            OB[k, rows, :] = norm_piece(H, EG, rows, r, (2 * oh + k) * SLICE + jj * CH, CH)
        own = pl.ds(pl.multiple_of(EROWS * b + 16 * i, 16), 16)
        for j in range(4):
            SB[j, rows, :] = norm_piece(H, EG, rows, r, (2 * h + 1 - c) * SLICE + j * CH, CH)
            XR[j, own, :] = norm_piece(H, EG, rows, r, b * SLICE + j * CH, CH)
        return 0

    def xr_rows(block, s):
        return pl.ds(pl.multiple_of(EROWS * block + HALF * s, 16), HALF)

    def half(s):
        return pl.ds(HALF * s, HALF)

    l_eg.wait()
    for s in range(2):
        l_h[s].wait()
        if s == 1:
            l_ph = load(ph, PH, 3)
            l_pg = load(pg, PG, 4)
            l_w = [load(w, W.at[:, pl.ds(HD * k, HD)], 5 + k) for k, w in enumerate((qw, kw, vw))]
        lax.fori_loop(5 * s, 5 * s + 5, ext_norm, 0)
        if s == 0:
            pl.semaphore_wait(barrier, len(everyone))
        for k in range(2):
            send(OB.at[k, half(s)], XR.at[jj, xr_rows(b, s)], r_pull.at[c, s], opp[k])
        send(SB.at[:, half(s)], XR.at[:, xr_rows(b, s)], r_sib.at[s], sib)

    l_kc = load(kc, KC, 8)
    l_vc = load(vc, VC, 9)
    l_pw = load(phead, PW, 10)
    l_small = [load(ids, IDS.at[pl.ds(0, CAND)], 11), load(clen, CL, 12), load(sh, SH, 13), load(prev, PV, 14)]

    l_ph.wait()
    l_pg.wait()

    def pol_norm(i, _):
        rows = pl.ds(pl.multiple_of(16 * i, 16), 16)
        own = pl.ds(pl.multiple_of(PROWS * b + 16 * i, 16), 16)
        r = row_scale(PH, rows)
        for j in range(4):
            for k in range(4):
                XP[j, own, pl.ds(CH * k, CH)] = norm_piece(PH, PG, rows, r, j * SLICE + k * CH, CH)
        return 0

    lax.fori_loop(0, 2, pol_norm, 0)

    def xp_rows(block):
        return pl.ds(pl.multiple_of(PROWS * block, 16), PROWS)

    own_p = xp_rows(b)

    def pass_on(s):
        region = XR.at[y, xr_rows(2 * oh, s)]
        got(region, r_pull.at[0, s])
        for k in (1, 3, 2):
            send(region, region, r_y.at[k - 1, s], ydev[k])
        region = XR.at[z % 4, xr_rows(2 * oh + 1, s)]
        got(region, r_pull.at[1, s])
        send(region, region, r_z.at[0, s], zdev[1])
        send(region, region, r_z.at[1, s], zdev[7])
        send(region, region, r_z.at[2, s], zdev[2 if s == 0 else 6])

    pass_on(0)
    send(XP.at[jj, own_p], XP.at[jj, own_p], r_pp, dev(1 - g, oh, y, z, c))
    send(XP.at[:, own_p], XP.at[:, own_p], r_psib, sib)

    for s in range(2):
        got(XR.at[:, xr_rows(2 * h + 1 - c, s)], r_sib.at[s])
    for cp in l_w:
        cp.wait()

    def project(rows):
        total = None
        for j in range(4):
            term = jnp.dot(XR[j, rows, :], W[pl.ds(CH * j, CH), :], preferred_element_type=F32)
            total = term if total is None else total + term
        return total

    def block_rows(block):
        return pl.ds(pl.multiple_of(EROWS * block, 16), EROWS)

    SO[...] = project(block_rows(2 * h + 1 - c))
    send(SO, RO, r_so, sib)
    ACC[...] = project(block_rows(b))

    pass_on(1)

    def arrive(s):
        for k in (1, 3, 2):
            got(XR.at[(y - k + 4) % 4, xr_rows(2 * oh, s)], r_y.at[k - 1, s])
        rows = xr_rows(2 * oh + 1, s)
        got(XR.at[(z + 7) % 4, rows], r_z.at[0, s])
        got(XR.at[(z + 1) % 4, rows], r_z.at[1, s])
        got(XR.at[(z + 2) % 4, rows], r_z.at[2, s])

    def exchange(s):
        arrive(s)
        ST[s] = project(xr_rows(2 * oh + 1 - c, s))
        send(ST.at[s], RT.at[s], r_st.at[s], sib)
        CS[s] = project(xr_rows(2 * oh + c, s))

    def cross(s):
        got(RT.at[s], r_st.at[s])
        CS[s] = CS[s] + RT[s]
        send(CS.at[s], CR.at[s], r_cr.at[s], xp_same)

    exchange(0)
    cross(0)

    pol_src = xp_rows(2 * oh + c)
    region = XP.at[jj, pol_src]
    got(region, r_pp)
    adev = [
        dev(g, h, (y + k * (1 - c)) % 4, (z + k * c) % 8, c) for k in (1, 7, 2, 6)
    ]
    lo = pl.ds(pl.multiple_of(PROWS * (2 * oh + c), 16), 16)
    hi = pl.ds(pl.multiple_of(PROWS * (2 * oh + c) + 16, 16), 16)
    send(region, region, r_pn.at[0], adev[0])
    send(region, region, r_pn.at[1], adev[1])
    send(XP.at[jj, lo], XP.at[jj, lo], r_pn.at[2], adev[2])
    send(XP.at[jj, hi], XP.at[jj, hi], r_pn.at[3], adev[3])
    send(region, region, r_pf.at[0], sib)

    exchange(1)
    cross(1)

    region = XP.at[(jj + 3) % 4, pol_src]
    got(region, r_pn.at[0])
    send(region, region, r_pf.at[1], sib)
    region = XP.at[(jj + 1) % 4, pol_src]
    got(region, r_pn.at[1])
    send(region, region, r_pf.at[2], sib)
    got(XP.at[(jj + 2) % 4, lo], r_pn.at[2])
    got(XP.at[(jj + 2) % 4, hi], r_pn.at[3])
    region = XP.at[(jj + 2) % 4, pol_src]
    send(region, region, r_pf.at[3], sib)

    for cp in l_small:
        cp.wait()
    l_kc.wait()
    l_vc.wait()
    got(RO, r_so)
    scale = 1.0 / HD**0.5
    slot = lax.broadcasted_iota(jnp.int32, (128, HALF), 0)
    src = lax.broadcasted_iota(jnp.int32, (128, HALF), 1)
    spread = jnp.where((src == (slot // 16) * CAND + slot % 16) & (slot % 16 < CAND), 1.0, 0.0).astype(BF16)
    r128 = lax.broadcasted_iota(jnp.int32, (128, 128), 0)
    l128 = lax.broadcasted_iota(jnp.int32, (128, 128), 1)
    position = lax.broadcasted_iota(jnp.int32, (128, CTX), 1)
    lens = jnp.pad(CL[...], ((0, 0), (0, 112)))

    def attend(s):
        got(CR.at[s], r_cr.at[s])
        qkv = (ACC[half(s), :] + RO[half(s), :] + CR[s]).astype(BF16)
        qkv = jnp.dot(spread, qkv, preferred_element_type=F32)
        query, key_new, value_new = qkv[:, :HD], qkv[:, HD : 2 * HD], qkv[:, 2 * HD :]
        own = jnp.sum(query * key_new, axis=1, keepdims=True) * scale
        q16 = query.astype(BF16)
        scores = jnp.concatenate(
            [
                lax.dot_general(
                    q16[16 * p : 16 * p + 16], KC[8 * s + p],
                    (((1,), (1,)), ((), ())), preferred_element_type=F32,
                )
                for p in range(8)
            ],
            axis=0,
        ) * scale
        length = jnp.sum(jnp.where(l128 == r128 // 16 + 8 * s, lens, 0), axis=1, keepdims=True)
        valid = position < length
        scores = jnp.where(valid, scores, -1e30)
        peak = jnp.maximum(jnp.max(scores, axis=1, keepdims=True), own)
        expo = jnp.where(valid, jnp.exp(scores - peak), 0.0)
        own_expo = jnp.exp(own - peak)
        whole = jnp.sum(expo, axis=1, keepdims=True) + own_expo
        weights = (expo / whole).astype(BF16)
        own_weight = (own_expo / whole).astype(BF16).astype(F32)
        attended = jnp.concatenate(
            [
                jnp.dot(weights[16 * p : 16 * p + 16], VC[8 * s + p], preferred_element_type=F32)
                for p in range(8)
            ],
            axis=0,
        )
        attended = attended + own_weight * value_new
        part = jnp.sum(attended * SH[...], axis=1, keepdims=True)
        return jnp.sum(jnp.where(r128 == l128, part, 0.0), axis=0, keepdims=True)

    reward0 = attend(0)

    got(XP.at[:, xp_rows(2 * h + 1 - c)], r_psib)
    sib_jj = y * c + (z % 4) * (1 - c)
    pol_sib = xp_rows(2 * oh + 1 - c)
    for k, shift in enumerate((0, 3, 1, 2)):
        got(XP.at[(sib_jj + shift) % 4, pol_sib], r_pf.at[k])
    l_pw.wait()

    def logits_step(j, total):
        w = PW[pl.ds(pl.multiple_of(SLICE * j, SLICE), SLICE), :]
        return total + jnp.dot(XP[j], w, preferred_element_type=F32)

    logits = lax.fori_loop(0, 4, logits_step, jnp.zeros((128, VOC), F32))
    first_col = ((g * 4 + b) * 32 + m) * VOC
    column = lax.broadcasted_iota(jnp.int32, (128, VOC), 1) + first_col
    peak = jnp.max(logits, axis=1, keepdims=True)
    stats = jnp.where(l128 == 0, peak, 0.0)
    stats = jnp.where(l128 == 1, jnp.sum(jnp.exp(logits - peak), axis=1, keepdims=True), stats)
    wanted = jnp.concatenate([IDS[...]] * 8, axis=0).T
    for k in range(CAND):
        pick = jnp.sum(jnp.where(column == wanted[:, k : k + 1], logits, 0.0), axis=1, keepdims=True)
        stats = jnp.where(l128 == 2 + k, pick, stats)
    R1[b] = stats.T[:16]
    for k, other in enumerate((sib, xp_same, xp_other)):
        send(R1.at[b], R1.at[b], r_1.at[k], other)

    reward1 = attend(1)

    sub16 = lax.broadcasted_iota(jnp.int32, (16, 128), 0)

    def merge(parts):
        top = functools.reduce(jnp.maximum, [t[0:1] for t in parts])
        total = None
        for t in parts:
            factor = jnp.where(sub16 == 1, jnp.exp(t[0:1] - top), 1.0)
            total = t * factor if total is None else total + t * factor
        return jnp.where(sub16 == 0, top, total)

    for k, other in enumerate((2 * h + 1 - c, 2 * oh + c, 2 * oh + 1 - c)):
        got(R1.at[other], r_1.at[k])
    me2 = g * 4 + y
    sub8 = lax.broadcasted_iota(jnp.int32, (8, 128), 0)
    R2[me2, 0:16] = merge([R1[k] for k in range(4)])
    R2[me2, 16:24] = jnp.where(sub8 == 0, reward0, jnp.where(sub8 == 1, reward1, 0.0))
    n = 0
    for k in range(4):
        for dg, devs in ((0, ydev), (1, gydev)):
            if k or dg:
                send(R2.at[me2], R2.at[me2], r_2.at[n], devs[k])
                n += 1
    n = 0
    for k in range(4):
        for dg in range(2):
            if k or dg:
                got(R2.at[(g + dg) % 2 * 4 + (y - k + 4) % 4], r_2.at[n])
                n += 1
    R3[z, 0:16] = merge([R2[k, 0:16] for k in range(8)])
    R3[z, 16:24] = functools.reduce(jnp.add, [R2[k, 16:24] for k in range(8)])
    for k in range(1, 8):
        send(R3.at[z], R3.at[z], r_3.at[k - 1], zdev[k])
    for k in range(1, 8):
        got(R3.at[(z - k + 8) % 8], r_3.at[k - 1])
    final = merge([R3[k, 0:16] for k in range(8)])
    reward = functools.reduce(jnp.add, [R3[k, 16:24] for k in range(8)])

    logprob = final - final[0:1] - jnp.log(final[1:2])
    mine = logprob
    for k in range(1, 4):
        mine = jnp.where(b == k, pltpu.roll(logprob, 128 - PROWS * k, 1), mine)
    lp_out[...] = mine[2 : 2 + CAND, :PROWS]
    both = jnp.where(sub16 < 8, reward[0:1], reward[1:2])
    spread_out = jnp.zeros((16, 128), F32)
    for k in range(8):
        spread_out = jnp.where(sub16 % 8 == k, pltpu.roll(both, (128 - 16 * k) % 128, 1), spread_out)
    rw_out[...] = spread_out[:, :CAND] + PV[...]

    for cp in sends:
        cp.wait_send()


def on_device(
    pol_hidden, pol_gain, pol_head, cand_ids, ext_hidden, ext_gain, query_w, key_w, value_w,
    key_cache, value_cache, cache_len, score_head, prev_logprob,
):
    vm = pltpu.VMEM
    dma = pltpu.SemaphoreType.DMA
    logprob, combined = pl.pallas_call(
        kernel,
        out_shape=(
            jax.ShapeDtypeStruct((CAND, PROWS), F32),
            jax.ShapeDtypeStruct((16, CAND), F32),
        ),
        in_specs=[pl.BlockSpec(memory_space=pl.ANY)] * 14,
        out_specs=(pl.BlockSpec(memory_space=vm), pl.BlockSpec(memory_space=vm)),
        scratch_shapes=[
            vm((EROWS, D), BF16),
            vm((1, D), F32),
            vm((PROWS, D), BF16),
            vm((1, D), F32),
            vm((D, VOC), BF16),
            vm((16, 128), jnp.int32),
            vm((SLICE, 3 * HD), BF16),
            vm((16, CTX, HD), BF16),
            vm((16, CTX, HD), BF16),
            vm((1, 16), jnp.int32),
            vm((1, HD), F32),
            vm((16, CAND), F32),
            vm((4, 4 * EROWS, CH), BF16),
            vm((4, EROWS, CH), BF16),
            vm((2, EROWS, CH), BF16),
            vm((4, 4 * PROWS, SLICE), BF16),
            vm((EROWS, 3 * HD), F32),
            vm((EROWS, 3 * HD), F32),
            vm((EROWS, 3 * HD), F32),
            vm((2, HALF, 3 * HD), F32),
            vm((2, HALF, 3 * HD), F32),
            vm((2, HALF, 3 * HD), F32),
            vm((2, HALF, 3 * HD), F32),
            vm((4, 16, 128), F32),
            vm((8, 24, 128), F32),
            vm((8, 24, 128), F32),
            dma((15,)),
            dma((64,)),
            dma((2, 2)),
            dma((2,)),
            dma((3, 2)),
            dma((3, 2)),
            dma,
            dma,
            dma((4,)),
            dma((4,)),
            dma,
            dma((2,)),
            dma((2,)),
            dma((3,)),
            dma((7,)),
            dma((7,)),
        ],
        compiler_params=pltpu.CompilerParams(
            collective_id=0, has_side_effects=True, vmem_limit_bytes=62 << 20
        ),
        name="candidates",
    )(
        pol_hidden, pol_gain.reshape(1, D), pol_head, cand_ids.T, ext_hidden, ext_gain.reshape(1, D),
        query_w, key_w, value_w, key_cache, value_cache, cache_len.reshape(1, 16),
        score_head.reshape(1, HD), prev_logprob,
    )
    return logprob.T, combined


def solution(mesh):
    placed = (
        P("batch", None),
        P(),
        P(None, ("group", "batch", "mp")),
        P(),
        P("batch", None),
        P(),
        P("batch", ("group", "mp")),
        P("batch", ("group", "mp")),
        P("batch", ("group", "mp")),
        P("batch", None, ("group", "mp")),
        P("batch", None, ("group", "mp")),
        P("batch"),
        P(("group", "mp")),
        P("batch", None),
    )
    return jax.shard_map(
        on_device,
        mesh=mesh,
        in_specs=placed,
        out_specs=(P("batch", None), P("batch", None)),
        check_vma=False,
    )
```

time: 392 us -> 52.2 us (0.13)
  blocking collectives: 326 us -> 0 us
  Pallas kernels: 0 us -> 48.8 us
  waiting for transfers between devices: 28.8 us -> 0 us
  matrix products: 14.7 us -> 0 us
  between operations: 13.9 us -> 0.64 us
  other arithmetic: 8.02 us -> 0 us
    psum x2 -> x0, blocking collectives: 234 us -> none  [the longest x1 159 us: on_device(): reward = lax.psum(partial_value, ('group', 'mp'))]
    pmax x1 -> x0, blocking collectives: 92 us -> none  [on_device(): top = lax.pmax(local_peak, ('group', 'batch', 'mp'))]
    pallas_call x0 -> x1, Pallas kernels: none -> 48.8 us  [on_device(): pl.pallas_call(kernel, out_shape=(jax.ShapeDtypeStruct((CAND, PROWS), F32...]
    all_gather x4 -> x0, waiting for transfers between devices: 26.9 us -> none  [the longest x1 26.8 us: on_device(): lax.all_gather(pol_normed, 'batch', axis=0, tiled=True)]
    dot_general x6 -> x0, matrix products: 14.7 us -> none  [the longest x3 10.3 us: on_device(): jnp.dot(ext_normed, weight_part, preferred_element_type=jnp.float32)]
    reduce_sum x5 -> x0, other arithmetic: 4.54 us -> none  [the longest x2 3.69 us: rms_norm(): spread = jnp.mean(values * values, axis=-1, keepdims=True)]
  transfers between devices with their start and end apart: 4 -> 0, of which waited for: 1 -> 0; matrix products, arithmetic and copies ran while one was open for 3% -> 0% of each run, Pallas kernels for 0% -> 0%
where the time goes in v1:
time: 52.2 us; the launch traced here: 52 us
  Pallas kernels  48.8 us (93%)
  local copies, waits for them, and re-layouts  2.59 us (5%)
  between operations  0.64 us (1%)
    pallas_call x1, Pallas kernels, on_device(): pl.pallas_call(kernel, out_shape=(jax.ShapeDtypeStruct((CAND, PROWS), F32...  48.8 us
    unnamed x2, local copies, waits for them, and re-layouts  2.59 us

profile of v1, /device:TPU:2, one launch (start us, length us, event | category | flops | bytes accessed | tf_op | source)
XLA Modules:
  0.0 52.0 jit_solution(18272704080931596163)
XLA Ops:
  0.6 48.8 %candidates.1 = (f32[10,32]{1,0:T(8,128)}, f32[16,10]{1,0:T(8,128)}) custom-call(bf16[32,8192]{1,0:T(8,128)(2,1)} %ph.1, f32[1,8192]{1,0:T(1,128)} %bitcast.6, bf16[8192,256]{1,0:T(8,128)(2,1)} %phead.1, s32[10,128]{1,0:T(8,128)} %bitcast.9, bf16[160,8192]{1,0:T(8,128)(2,1)} %eh.1, f32[1,8192]{1,0:T(1,128)} %bitcast.7, bf16[2048,128]{1,0:T(8,128)(2,1)} %qw.1, ...), custom_call_target="tpu_custom_call" | custom-call | tf_op jit(solution)/shard_map/candidates/pallas_call | solution.py:369
  49.4 1.3 %copy.18 = f32[32,10]{0,1:T(8,128)} copy(f32[32,10]{0,1:T(8,128)} %bitcast.8) | data formatting | bytes 2560
  50.7 1.3 %copy.19 = f32[16,10]{1,0:T(8,128)} copy(f32[16,10]{1,0:T(8,128)} %get-tuple-element.9) | data formatting | bytes 1280

commit v2 on v1

v2 whole, which is shorter than its diff:
```python
import functools

import jax
import jax.numpy as jnp
from jax import lax
from jax.experimental import pallas as pl
from jax.experimental.pallas import tpu as pltpu
from jax.sharding import PartitionSpec as P

MESH = pl.DeviceIdType.MESH
F32 = jnp.float32
BF16 = jnp.bfloat16

D = 8192
HD = 128
CAND = 10
CTX = 256
EROWS = 160
HALF = 80
PROWS = 32
SLICE = 2048
CH = 512
VOC = 256
PART = 32
PARTS = 5


def part(q):
    return pl.ds(PART * q, PART)


def kernel(
    ph, pg, phead, ids, eh, eg, qw, kw, vw, kc, vc, clen, sh, prev,
    out,
    H, EG, PH, PG, PW, IDS, W, KC, VC, CL, SH, PV,
    XR, SB, OB, XP, ACC, SO, RO, ST, RT, CS, CB, CR, R1, Q, S,
    lsem, ssem, r_pull, r_sib, r_y, r_z, r_psib, r_pp, r_pn, r_pf, r_so, r_st, r_cr,
    r_1, r_q, s_q, r_s, s_s, met2, met3,
):
    g = lax.axis_index("group")
    b = lax.axis_index("batch")
    m = lax.axis_index("mp")
    y, z, h, c = m % 4, m // 4, b // 2, b % 2
    oh = 1 - h

    def dev(dg, dh, y_, z_, c_):
        return (dg, 2 * dh + c_, 4 * z_ + y_)

    sib = dev(g, h, y, z, 1 - c)
    opp = [dev(1 - g, oh, y, z, k) for k in range(2)]
    xp_same = dev(g, oh, y, z, c)
    xp_other = dev(g, oh, y, z, 1 - c)
    ydev = [dev(g, h, (y + k) % 4, z, c) for k in range(4)]
    gydev = [dev(1 - g, h, (y + k) % 4, z, c) for k in range(4)]
    zdev = [dev(g, h, y, (z + k) % 8, c) for k in range(8)]

    def load(src, dst, k):
        cp = pltpu.make_async_copy(src, dst, lsem.at[k])
        cp.start()
        return cp

    l_eg = load(eg, EG, 2)
    l_h = [load(eh.at[part(q)], H.at[part(q)], 3 + q) for q in range(PARTS)]
    l_ph = load(ph, PH, 0)
    l_pg = load(pg, PG, 1)

    near = [sib, *opp, xp_same, xp_other, *gydev, *ydev[1:], zdev[1], zdev[2], zdev[6], zdev[7]]
    barrier = pltpu.get_barrier_semaphore()
    for other in near:
        pl.semaphore_signal(barrier, inc=1, device_id=other, device_id_type=MESH)

    sends = []

    def send(src, dst, rsem, target):
        cp = pltpu.make_async_remote_copy(
            src_ref=src, dst_ref=dst, send_sem=ssem.at[len(sends)], recv_sem=rsem,
            device_id=target, device_id_type=MESH,
        )
        cp.start()
        sends.append(cp)

    def got(region, rsem):
        pltpu.make_async_copy(region, region, rsem).wait()

    def row_scale(ref, rows):
        acc = jnp.zeros((16, 512), F32)
        for k in range(D // 512):
            v = ref[rows, pl.ds(512 * k, 512)].astype(F32)
            acc = acc + v * v
        mean = jnp.sum(acc, axis=1, keepdims=True) * (1.0 / D)
        return lax.rsqrt(mean + 1e-05)

    jj = y * (1 - c) + (z % 4) * c

    def norm_piece(ref, gain, rows, r, start, width):
        cols = pl.ds(pl.multiple_of(start, 128), width)
        return (ref[rows, cols].astype(F32) * r * gain[:, cols]).astype(BF16)

    def pol_norm(i, _):
        rows = pl.ds(pl.multiple_of(16 * i, 16), 16)
        own = pl.ds(pl.multiple_of(PROWS * b + 16 * i, 16), 16)
        r = row_scale(PH, rows)
        for j in range(4):
            for k in range(4):
                XP[j, own, pl.ds(CH * k, CH)] = norm_piece(PH, PG, rows, r, j * SLICE + k * CH, CH)
        return 0

    def xp_rows(block):
        return pl.ds(pl.multiple_of(PROWS * block, 16), PROWS)

    def xp_half(block, e):
        return pl.ds(pl.multiple_of(PROWS * block + 16 * e, 16), 16)

    def greet(sem):
        for other in near:
            pl.semaphore_signal(sem, inc=1, device_id=other, device_id_type=MESH)

    def ext_norm(i, _):
        rows = pl.ds(pl.multiple_of(16 * i, 16), 16)
        r = row_scale(H, rows)
        for k in range(2):
            OB[k, rows, :] = norm_piece(H, EG, rows, r, (2 * oh + k) * SLICE + jj * CH, CH)
        own = pl.ds(pl.multiple_of(EROWS * b + 16 * i, 16), 16)
        for j in range(4):
            SB[j, rows, :] = norm_piece(H, EG, rows, r, (2 * h + 1 - c) * SLICE + j * CH, CH)
            XR[j, own, :] = norm_piece(H, EG, rows, r, b * SLICE + j * CH, CH)
        return 0

    def xr_rows(block, q):
        return pl.ds(pl.multiple_of(EROWS * block + PART * q, 16), PART)

    def xr_block(block):
        return pl.ds(pl.multiple_of(EROWS * block, 16), EROWS)

    l_eg.wait()
    for q in range(PARTS):
        l_h[q].wait()
        lax.fori_loop(2 * q, 2 * q + 2, ext_norm, 0)
        if q == 0:
            pl.semaphore_wait(barrier, len(near))
            greet(met2)
        for k in range(2):
            send(OB.at[k, part(q)], XR.at[jj, xr_rows(b, q)], r_pull.at[c, q], opp[k])
    send(SB, XR.at[:, xr_block(b)], r_sib, sib)
    l_w = [load(w, W.at[:, pl.ds(HD * k, HD)], 8 + k) for k, w in enumerate((qw, kw, vw))]

    l_ph.wait()
    l_pg.wait()
    lax.fori_loop(0, 2, pol_norm, 0)
    for e in range(2):
        piece = XP.at[jj, xp_half(b, e)]
        send(piece, piece, r_pp.at[e], dev(1 - g, oh, y, z, c))
    own_p = XP.at[:, xp_rows(b)]
    send(own_p, own_p, r_psib, sib)

    l_pw = load(phead, PW, 11)
    l_kc = load(kc, KC, 12)
    l_vc = load(vc, VC, 13)
    l_small = [
        load(ids, IDS.at[pl.ds(0, CAND)], 14), load(clen, CL, 15), load(sh, SH, 16), load(prev, PV, 17)
    ]

    def project(*pieces):
        total = None
        for j in range(4):
            x = [XR[j, rows, :] for rows in pieces]
            x = x[0] if len(x) == 1 else jnp.concatenate(x, axis=0)
            term = jnp.dot(x, W[pl.ds(CH * j, CH), :], preferred_element_type=F32)
            total = term if total is None else total + term
        return total

    for cp in l_w:
        cp.wait()
    got(XR.at[:, xr_block(2 * h + 1 - c)], r_sib)
    both = project(xr_block(2 * h + 1 - c), xr_block(b))
    SO[...] = both[:EROWS]
    send(SO, RO, r_so, sib)
    ACC[...] = both[EROWS:]

    pl.semaphore_wait(met2, len(near))
    greet(met3)

    pol_src = 2 * oh + c
    adev = [
        dev(g, h, (y + k * (1 - c)) % 4, (z + k * c) % 8, c) for k in (1, 7, 2, 6)
    ]
    def pol_on(e):
        piece = XP.at[jj, xp_half(pol_src, e)]
        got(piece, r_pp.at[e])
        send(piece, piece, r_pn.at[2, e], adev[2 + e])
        send(piece, piece, r_pn.at[0, e], adev[0])
        send(piece, piece, r_pn.at[1, e], adev[1])
        if e == 1:
            piece = XP.at[jj, xp_rows(pol_src)]
            send(piece, piece, r_pf.at[0], sib)

    def pol_pass(k):
        j = (jj + (3, 1, 2)[k]) % 4
        for e in range(2):
            got(XP.at[j, xp_half(pol_src, e)], r_pn.at[k, e])
        piece = XP.at[j, xp_rows(pol_src)]
        send(piece, piece, r_pf.at[k + 1], sib)

    def pass_on(q):
        piece = XR.at[y, xr_rows(2 * oh, q)]
        got(piece, r_pull.at[0, q])
        for k in (2, 1, 3):
            send(piece, piece, r_y.at[k - 1, q], ydev[k])
        piece = XR.at[z % 4, xr_rows(2 * oh + 1, q)]
        got(piece, r_pull.at[1, q])
        send(piece, piece, r_z.at[2, q], zdev[2 if q % 2 == 0 else 6])
        send(piece, piece, r_z.at[0, q], zdev[1])
        send(piece, piece, r_z.at[1, q], zdev[7])

    def exchange(q):
        for k in (1, 3, 2):
            got(XR.at[(y - k + 4) % 4, xr_rows(2 * oh, q)], r_y.at[k - 1, q])
        rows = xr_rows(2 * oh + 1, q)
        got(XR.at[(z + 7) % 4, rows], r_z.at[0, q])
        got(XR.at[(z + 1) % 4, rows], r_z.at[1, q])
        got(XR.at[(z + 2) % 4, rows], r_z.at[2, q])
        both = project(xr_rows(2 * oh + 1 - c, q), xr_rows(2 * oh + c, q))
        ST[q] = both[:PART]
        send(ST.at[q], RT.at[q], r_st.at[q], sib)
        CS[q] = both[PART:]

    def cross(q):
        got(RT.at[q], r_st.at[q])
        total = CS[q] + RT[q]
        query = total[:, :HD]
        high = query.astype(BF16)
        CB[q, :, 0:HD] = high
        CB[q, :, HD : 2 * HD] = (query - high.astype(F32)).astype(BF16)
        CB[q, :, 2 * HD :] = total[:, HD:].astype(BF16)
        send(CB.at[q], CR.at[q], r_cr.at[q], xp_same)

    for q in range(4):
        pass_on(q)
    exchange(0)
    pass_on(4)
    exchange(1)
    cross(0)
    exchange(2)
    cross(1)
    pol_on(0)
    exchange(3)
    cross(2)
    pol_on(1)
    exchange(4)
    cross(3)
    pol_pass(0)
    cross(4)
    pol_pass(1)
    pol_pass(2)
    pl.semaphore_wait(met3, len(near))

    for cp in l_small:
        cp.wait()
    l_kc.wait()
    l_vc.wait()

    scale = 1.0 / HD**0.5
    slot = lax.broadcasted_iota(jnp.int32, (128, HALF), 0)
    src = lax.broadcasted_iota(jnp.int32, (128, HALF), 1)
    spread = jnp.where((src == (slot // 16) * CAND + slot % 16) & (slot % 16 < CAND), 1.0, 0.0).astype(BF16)
    r128 = lax.broadcasted_iota(jnp.int32, (128, 128), 0)
    l128 = lax.broadcasted_iota(jnp.int32, (128, 128), 1)
    position = lax.broadcasted_iota(jnp.int32, (128, CTX), 1)
    lens = jnp.pad(CL[...], ((0, 0), (0, 112)))

    def attend(s):
        if s == 0:
            pieces = [CR[0], CR[1], CR[2, 0:16]]
        else:
            pieces = [CR[2, 16:32], CR[3], CR[4]]
        got_rows = jnp.concatenate(pieces, axis=0).astype(F32)
        got_rows = jnp.concatenate(
            [got_rows[:, :HD] + got_rows[:, HD : 2 * HD], got_rows[:, 2 * HD :]], axis=1
        )
        mine = pl.ds(HALF * s, HALF)
        qkv = (ACC[mine, :] + RO[mine, :] + got_rows).astype(BF16)
        qkv = jnp.dot(spread, qkv, preferred_element_type=F32)
        query, key_new, value_new = qkv[:, :HD], qkv[:, HD : 2 * HD], qkv[:, 2 * HD :]
        own = jnp.sum(query * key_new, axis=1, keepdims=True) * scale
        q16 = query.astype(BF16)
        scores = jnp.concatenate(
            [
                lax.dot_general(
                    q16[16 * p : 16 * p + 16], KC[8 * s + p],
                    (((1,), (1,)), ((), ())), preferred_element_type=F32,
                )
                for p in range(8)
            ],
            axis=0,
        ) * scale
        length = jnp.sum(jnp.where(l128 == r128 // 16 + 8 * s, lens, 0), axis=1, keepdims=True)
        valid = position < length
        scores = jnp.where(valid, scores, -1e30)
        peak = jnp.maximum(jnp.max(scores, axis=1, keepdims=True), own)
        expo = jnp.where(valid, jnp.exp(scores - peak), 0.0)
        own_expo = jnp.exp(own - peak)
        whole = jnp.sum(expo, axis=1, keepdims=True) + own_expo
        weights = (expo / whole).astype(BF16)
        own_weight = (own_expo / whole).astype(BF16).astype(F32)
        attended = jnp.concatenate(
            [
                jnp.dot(weights[16 * p : 16 * p + 16], VC[8 * s + p], preferred_element_type=F32)
                for p in range(8)
            ],
            axis=0,
        )
        attended = attended + own_weight * value_new
        total = jnp.sum(attended * SH[...], axis=1, keepdims=True)
        return jnp.sum(jnp.where(r128 == l128, total, 0.0), axis=0, keepdims=True)

    got(RO, r_so)
    for q in range(3):
        got(CR.at[q], r_cr.at[q])
    reward0 = attend(0)

    got(XP.at[:, xp_rows(2 * h + 1 - c)], r_psib)
    sib_jj = y * c + (z % 4) * (1 - c)
    for k, shift in enumerate((0, 3, 1, 2)):
        got(XP.at[(sib_jj + shift) % 4, xp_rows(2 * oh + 1 - c)], r_pf.at[k])
    l_pw.wait()
    logits = None
    for j in range(4):
        term = jnp.dot(XP[j], PW[pl.ds(SLICE * j, SLICE), :], preferred_element_type=F32)
        logits = term if logits is None else logits + term
    first_col = ((g * 4 + b) * 32 + m) * VOC
    logits = logits.T
    column = lax.broadcasted_iota(jnp.int32, (VOC, 128), 0) + first_col
    wanted = IDS[...]
    peak = jnp.max(logits, axis=0, keepdims=True)
    stats = [peak, jnp.sum(jnp.exp(logits - peak), axis=0, keepdims=True)]
    for k in range(CAND):
        stats.append(jnp.sum(jnp.where(column == wanted[k : k + 1, :], logits, 0.0), axis=0, keepdims=True))
    R1[b] = jnp.concatenate([*stats, jnp.zeros((4, 128), F32)], axis=0)
    for k, other in enumerate((sib, xp_same, xp_other)):
        send(R1.at[b], R1.at[b], r_1.at[k], other)

    me = g * 32 + y * 8 + z

    def spread_far(buf, rsem, sem):
        def far(o):
            return -(o[0] + min(o[1], 4 - o[1]) + min(o[2], 8 - o[2]))

        offsets = [(i, j, k) for i in range(2) for j in range(4) for k in range(8) if i or j or k]
        for i, j, k in sorted(offsets, key=far):
            pltpu.make_async_remote_copy(
                src_ref=buf.at[me], dst_ref=buf.at[me], send_sem=sem, recv_sem=rsem,
                device_id=dev((g + i) % 2, h, (y + j) % 4, (z + k) % 8, c), device_id_type=MESH,
            ).start()

    for q in range(3, PARTS):
        got(CR.at[q], r_cr.at[q])
    reward1 = attend(1)
    Q[me] = jnp.concatenate([reward0, reward1], axis=0)
    spread_far(Q, r_q, s_q)

    sub16 = lax.broadcasted_iota(jnp.int32, (16, 128), 0)

    def merge(parts):
        top = functools.reduce(jnp.maximum, [t[0:1] for t in parts])
        total = None
        for t in parts:
            factor = jnp.where(sub16 == 1, jnp.exp(t[0:1] - top), 1.0)
            total = t * factor if total is None else total + t * factor
        return jnp.where(sub16 == 0, top, total)

    for k, other in enumerate((2 * h + 1 - c, 2 * oh + c, 2 * oh + 1 - c)):
        got(R1.at[other], r_1.at[k])
    total = merge([R1[k] for k in range(4)])
    mine = total
    for k in range(1, 4):
        mine = jnp.where(b == k, pltpu.roll(total, 128 - PROWS * k, 1), mine)
    lane4 = lax.broadcasted_iota(jnp.int32, (4, 128), 1) // PROWS
    packed = jnp.zeros((4, 128), F32)
    for k in range(4):
        rows = jnp.concatenate([mine[4 * r + k : 4 * r + k + 1] for r in range(4)], axis=0)
        packed = jnp.where(lane4 == k, pltpu.roll(rows, PROWS * k, 1) if k else rows, packed)
    S[me] = packed
    spread_far(S, r_s, s_s)

    for cp in sends:
        cp.wait_send()
    others = pl.ds(0, 63)
    got(Q.at[others], r_q)
    reward = jnp.sum(Q[...], axis=0)
    both = jnp.where(sub16 < 8, reward[0:1], reward[1:2])
    spread_out = jnp.zeros((16, 128), F32)
    for k in range(8):
        spread_out = jnp.where(sub16 % 8 == k, pltpu.roll(both, (128 - 16 * k) % 128, 1), spread_out)
    out[16:32, :] = spread_out + jnp.pad(PV[...], ((0, 0), (0, 128 - CAND)))
    got(Q.at[others], s_q)

    got(S.at[others], r_s)
    first = S[:, 0, :]
    lane1 = lax.broadcasted_iota(jnp.int32, (1, 128), 1) // PROWS
    lane64 = lax.broadcasted_iota(jnp.int32, (64, 128), 1) // PROWS
    top = jnp.max(first, axis=0, keepdims=True)
    factor = pltpu.roll(jnp.exp(first - top), PROWS, 1)
    first = jnp.sum(jnp.where(lane64 == 1, first * factor, first), axis=0, keepdims=True)
    total = jnp.sum(S[...], axis=0)
    total = jnp.concatenate([first, total[1:]], axis=0)
    log_total = pltpu.roll(jnp.log(jnp.where(lane1 == 1, first, 1.0)), 128 - PROWS, 1)

    def over_lanes(v):
        v = jnp.where(lane1 == 0, v, 0.0)
        return functools.reduce(jnp.add, [pltpu.roll(v, PROWS * k, 1) if k else v for k in range(4)])

    total = total - over_lanes(top) - over_lanes(log_total)
    for k in range(CAND):
        r, k4 = (k + 2) // 4, (k + 2) % 4
        row = total[r : r + 1]
        out[k : k + 1, :] = pltpu.roll(row, 128 - PROWS * k4, 1) if k4 else row
    got(S.at[others], s_s)


def place(packed, lp_out, rw_out, x, sem):
    cp = pltpu.make_async_copy(packed, x, sem)
    cp.start()
    cp.wait()
    lp_out[...] = x[0:CAND, :PROWS]
    rw_out[...] = x[16:32, :CAND]


def on_device(
    pol_hidden, pol_gain, pol_head, cand_ids, ext_hidden, ext_gain, query_w, key_w, value_w,
    key_cache, value_cache, cache_len, score_head, prev_logprob,
):
    vm = pltpu.VMEM
    dma = pltpu.SemaphoreType.DMA
    packed = pl.pallas_call(
        kernel,
        out_shape=jax.ShapeDtypeStruct((32, 128), F32),
        in_specs=[pl.BlockSpec(memory_space=pl.ANY)] * 14,
        out_specs=pl.BlockSpec(memory_space=vm),
        scratch_shapes=[
            vm((EROWS, D), BF16),
            vm((1, D), F32),
            vm((PROWS, D), BF16),
            vm((1, D), F32),
            vm((D, VOC), BF16),
            vm((16, 128), jnp.int32),
            vm((SLICE, 3 * HD), BF16),
            vm((16, CTX, HD), BF16),
            vm((16, CTX, HD), BF16),
            vm((1, 16), jnp.int32),
            vm((1, HD), F32),
            vm((16, CAND), F32),
            vm((4, 4 * EROWS, CH), BF16),
            vm((4, EROWS, CH), BF16),
            vm((2, EROWS, CH), BF16),
            vm((4, 4 * PROWS, SLICE), BF16),
            vm((EROWS, 3 * HD), F32),
            vm((EROWS, 3 * HD), F32),
            vm((EROWS, 3 * HD), F32),
            vm((PARTS, PART, 3 * HD), F32),
            vm((PARTS, PART, 3 * HD), F32),
            vm((PARTS, PART, 3 * HD), F32),
            vm((PARTS, PART, 4 * HD), BF16),
            vm((PARTS, PART, 4 * HD), BF16),
            vm((4, 16, 128), F32),
            vm((64, 2, 128), F32),
            vm((64, 4, 128), F32),
            dma((18,)),
            dma((128,)),
            dma((2, PARTS)),
            dma,
            dma((3, PARTS)),
            dma((3, PARTS)),
            dma,
            dma((2,)),
            dma((3, 2)),
            dma((4,)),
            dma,
            dma((PARTS,)),
            dma((PARTS,)),
            dma((3,)),
            dma,
            dma,
            dma,
            dma,
            pltpu.SemaphoreType.REGULAR,
            pltpu.SemaphoreType.REGULAR,
        ],
        compiler_params=pltpu.CompilerParams(
            collective_id=0, has_side_effects=True, vmem_limit_bytes=62 << 20
        ),
        name="candidates",
    )(
        pol_hidden, pol_gain.reshape(1, D), pol_head, cand_ids.T, ext_hidden, ext_gain.reshape(1, D),
        query_w, key_w, value_w, key_cache, value_cache, cache_len.reshape(1, 16),
        score_head.reshape(1, HD), prev_logprob,
    )
    logprob, combined = pl.pallas_call(
        place,
        out_shape=(
            jax.ShapeDtypeStruct((CAND, PROWS), F32),
            jax.ShapeDtypeStruct((16, CAND), F32),
        ),
        in_specs=[pl.BlockSpec(memory_space=pl.ANY)],
        scratch_shapes=[vm((32, 128), F32), dma],
        compiler_params=pltpu.CompilerParams(vmem_limit_bytes=62 << 20),
        name="place",
    )(packed)
    return logprob.T, combined


def solution(mesh):
    placed = (
        P("batch", None),
        P(),
        P(None, ("group", "batch", "mp")),
        P(),
        P("batch", None),
        P(),
        P("batch", ("group", "mp")),
        P("batch", ("group", "mp")),
        P("batch", ("group", "mp")),
        P("batch", None, ("group", "mp")),
        P("batch", None, ("group", "mp")),
        P("batch"),
        P(("group", "mp")),
        P("batch", None),
    )
    return jax.shard_map(
        on_device,
        mesh=mesh,
        in_specs=placed,
        out_specs=(P("batch", None), P("batch", None)),
        check_vma=False,
    )
```

time: 52.2 us -> 45.6 us (0.87); the launches traced: 52 us -> 44.8 us
  Pallas kernels: 48.8 us -> 44.1 us
  local copies, waits for them, and re-layouts: 2.59 us -> 0 us
    pallas_call x1 -> x2, Pallas kernels: 48.8 us -> 44.1 us  [the longest x1 42.8 us: on_device(): pl.pallas_call(kernel, out_shape=jax.ShapeDtypeStruct((32, 128), F32), in...]
    unnamed x2 -> x0, local copies, waits for them, and re-layouts: 2.59 us -> none
where the time goes in v2:
time: 45.6 us; the launch traced here: 44.8 us
  Pallas kernels  44.1 us (97%)
  between operations  0.64 us (1%)
    pallas_call x1, Pallas kernels, on_device(): pl.pallas_call(kernel, out_shape=jax.ShapeDtypeStruct((32, 128), F32), in...  42.8 us
    pallas_call x1, Pallas kernels, on_device(): pl.pallas_call(place, out_shape=(jax.ShapeDtypeStruct((CAND, PROWS), F32)...  1.33 us

profile of v2, /device:TPU:2, one launch (start us, length us, event | category | flops | bytes accessed | tf_op | source)
XLA Modules:
  0.0 44.8 jit_solution(1213452162980404888)
XLA Ops:
  0.6 42.8 %candidates.1.packed = f32[32,128]{1,0:T(8,128)} custom-call(bf16[32,8192]{1,0:T(8,128)(2,1)} %ph.1, f32[1,8192]{1,0:T(1,128)} %bitcast.6, bf16[8192,256]{1,0:T(8,128)(2,1)} %phead.1, s32[10,128]{1,0:T(8,128)} %bitcast.8, bf16[160,8192]{1,0:T(8,128)(2,1)} %eh.1, f32[1,8192]{1,0:T(1,128)} %bitcast.7, bf16[2048,128]{1,0:T(8,128)(2,1)} %qw.1, ...), custom_call_target="tpu_custom_call" | custom-call | tf_op jit(solution)/shard_map/candidates/pallas_call | solution.py:434
  43.5 1.3 %place.1 = (f32[10,32]{1,0:T(8,128)}, f32[16,10]{1,0:T(8,128)}) custom-call(f32[32,128]{1,0:T(8,128)} %candidates.1.packed), custom_call_target="tpu_custom_call" | custom-call | tf_op jit(solution)/shard_map/place/pallas_call | solution.py:497

commit v3 on v2

--- a/solution.py
+++ b/solution.py
@@ -21,21 +21,23 @@
 SLICE = 2048
 CH = 512
 VOC = 256
-PART = 32
-PARTS = 5
+STARTS = (0, 16, 48, 80, 112, 144)
+SIZES = (16, 32, 32, 32, 32, 16)
+PARTS = 6
+LAST = PARTS - 1
 
 
 def part(q):
-    return pl.ds(PART * q, PART)
+    return pl.ds(STARTS[q], SIZES[q])
 
 
 def kernel(
     ph, pg, phead, ids, eh, eg, qw, kw, vw, kc, vc, clen, sh, prev,
     out,
     H, EG, PH, PG, PW, IDS, W, KC, VC, CL, SH, PV,
-    XR, SB, OB, XP, ACC, SO, RO, ST, RT, CS, CB, CR, R1, Q, S,
-    lsem, ssem, r_pull, r_sib, r_y, r_z, r_psib, r_pp, r_pn, r_pf, r_so, r_st, r_cr,
-    r_1, r_q, s_q, r_s, s_s, met2, met3,
+    XR, SB, OB, XP, ACC, SO, RO, ST, RT, CS, CB, CR, CB2, CR2, R1, Q, S,
+    lsem, ssem, r_pull, r_sib, r_y, r_z, r_psib, r_pp, r_pn, r_pf, r_so, r_st, r_cr, r_cr2,
+    r_1, s_1, r_q, s_q, r_s, s_s, met2, met3, met4,
 ):
     g = lax.axis_index("group")
     b = lax.axis_index("batch")
@@ -59,12 +61,12 @@
         cp.start()
         return cp
 
-    l_eg = load(eg, EG, 2)
-    l_h = [load(eh.at[part(q)], H.at[part(q)], 3 + q) for q in range(PARTS)]
     l_ph = load(ph, PH, 0)
     l_pg = load(pg, PG, 1)
-
-    near = [sib, *opp, xp_same, xp_other, *gydev, *ydev[1:], zdev[1], zdev[2], zdev[6], zdev[7]]
+    l_eg = load(eg, EG, 2)
+    near = [sib, *opp, gydev[0], ydev[1], ydev[3], zdev[1], zdev[7]]
+    near2 = [*near, ydev[2], zdev[2], zdev[6]]
+    planes = [*ydev[1:], *gydev]
     barrier = pltpu.get_barrier_semaphore()
     for other in near:
         pl.semaphore_signal(barrier, inc=1, device_id=other, device_id_type=MESH)
@@ -111,9 +113,21 @@
     def xp_half(block, e):
         return pl.ds(pl.multiple_of(PROWS * block + 16 * e, 16), 16)
 
-    def greet(sem):
-        for other in near:
+    def greet(sem, others):
+        for other in others:
             pl.semaphore_signal(sem, inc=1, device_id=other, device_id_type=MESH)
+
+    l_ph.wait()
+    l_pg.wait()
+    l_h = [load(eh.at[part(q)], H.at[part(q)], 3 + q) for q in range(PARTS)]
+    lax.fori_loop(0, 2, pol_norm, 0)
+    pl.semaphore_wait(barrier, len(near))
+    greet(met2, near)
+    for e in range(2):
+        piece = XP.at[jj, xp_half(b, e)]
+        send(piece, piece, r_pp.at[e], dev(1 - g, oh, y, z, c))
+    own_p = XP.at[:, xp_rows(b)]
+    send(own_p, own_p, r_psib, sib)
 
     def ext_norm(i, _):
         rows = pl.ds(pl.multiple_of(16 * i, 16), 16)
@@ -127,37 +141,29 @@
         return 0
 
     def xr_rows(block, q):
-        return pl.ds(pl.multiple_of(EROWS * block + PART * q, 16), PART)
+        return pl.ds(pl.multiple_of(EROWS * block + STARTS[q], 16), SIZES[q])
 
     def xr_block(block):
         return pl.ds(pl.multiple_of(EROWS * block, 16), EROWS)
 
     l_eg.wait()
+    def pull(q):
+        for k in range(2):
+            send(OB.at[k, part(q)], XR.at[jj, xr_rows(b, q)], r_pull.at[c, q], opp[k])
+
     for q in range(PARTS):
         l_h[q].wait()
-        lax.fori_loop(2 * q, 2 * q + 2, ext_norm, 0)
-        if q == 0:
-            pl.semaphore_wait(barrier, len(near))
-            greet(met2)
-        for k in range(2):
-            send(OB.at[k, part(q)], XR.at[jj, xr_rows(b, q)], r_pull.at[c, q], opp[k])
+        lax.fori_loop(STARTS[q] // 16, (STARTS[q] + SIZES[q]) // 16, ext_norm, 0)
+        if q < 2:
+            pull(q)
     send(SB, XR.at[:, xr_block(b)], r_sib, sib)
-    l_w = [load(w, W.at[:, pl.ds(HD * k, HD)], 8 + k) for k, w in enumerate((qw, kw, vw))]
-
-    l_ph.wait()
-    l_pg.wait()
-    lax.fori_loop(0, 2, pol_norm, 0)
-    for e in range(2):
-        piece = XP.at[jj, xp_half(b, e)]
-        send(piece, piece, r_pp.at[e], dev(1 - g, oh, y, z, c))
-    own_p = XP.at[:, xp_rows(b)]
-    send(own_p, own_p, r_psib, sib)
-
-    l_pw = load(phead, PW, 11)
-    l_kc = load(kc, KC, 12)
-    l_vc = load(vc, VC, 13)
+    l_w = [load(w, W.at[:, pl.ds(HD * k, HD)], 9 + k) for k, w in enumerate((qw, kw, vw))]
+
+    l_pw = load(phead, PW, 12)
+    l_kc = load(kc, KC, 13)
+    l_vc = load(vc, VC, 14)
     l_small = [
-        load(ids, IDS.at[pl.ds(0, CAND)], 14), load(clen, CL, 15), load(sh, SH, 16), load(prev, PV, 17)
+        load(ids, IDS.at[pl.ds(0, CAND)], 15), load(clen, CL, 16), load(sh, SH, 17), load(prev, PV, 18)
     ]
 
     def project(*pieces):
@@ -178,7 +184,7 @@
     ACC[...] = both[EROWS:]
 
     pl.semaphore_wait(met2, len(near))
-    greet(met3)
+    greet(met3, near2)
 
     pol_src = 2 * oh + c
     adev = [
@@ -212,7 +218,7 @@
         send(piece, piece, r_z.at[0, q], zdev[1])
         send(piece, piece, r_z.at[1, q], zdev[7])
 
-    def exchange(q):
+    def ready(q):
         for k in (1, 3, 2):
             got(XR.at[(y - k + 4) % 4, xr_rows(2 * oh, q)], r_y.at[k - 1, q])
         rows = xr_rows(2 * oh + 1, q)
@@ -220,44 +226,36 @@
         got(XR.at[(z + 1) % 4, rows], r_z.at[1, q])
         got(XR.at[(z + 2) % 4, rows], r_z.at[2, q])
         both = project(xr_rows(2 * oh + 1 - c, q), xr_rows(2 * oh + c, q))
-        ST[q] = both[:PART]
-        send(ST.at[q], RT.at[q], r_st.at[q], sib)
-        CS[q] = both[PART:]
-
-    def cross(q):
-        got(RT.at[q], r_st.at[q])
-        total = CS[q] + RT[q]
+        return both[: SIZES[q]], both[SIZES[q] :]
+
+    def exchange(q):
+        theirs, ours = ready(q)
+        ST[part(q), :] = theirs
+        send(ST.at[part(q)], RT.at[part(q)], r_st.at[q], sib)
+        CS[part(q), :] = ours
+
+    def split(ref, rows, total):
         query = total[:, :HD]
         high = query.astype(BF16)
-        CB[q, :, 0:HD] = high
-        CB[q, :, HD : 2 * HD] = (query - high.astype(F32)).astype(BF16)
-        CB[q, :, 2 * HD :] = total[:, HD:].astype(BF16)
-        send(CB.at[q], CR.at[q], r_cr.at[q], xp_same)
-
-    for q in range(4):
-        pass_on(q)
-    exchange(0)
-    pass_on(4)
-    exchange(1)
-    cross(0)
-    exchange(2)
-    cross(1)
-    pol_on(0)
-    exchange(3)
-    cross(2)
-    pol_on(1)
-    exchange(4)
-    cross(3)
-    pol_pass(0)
-    cross(4)
-    pol_pass(1)
-    pol_pass(2)
-    pl.semaphore_wait(met3, len(near))
+        ref[rows, 0:HD] = high
+        ref[rows, HD : 2 * HD] = (query - high.astype(F32)).astype(BF16)
+        ref[rows, 2 * HD :] = total[:, HD:].astype(BF16)
+
+    def cross(q):
+        got(RT.at[part(q)], r_st.at[q])
+        split(CB, part(q), CS[part(q), :] + RT[part(q), :])
+        send(CB.at[part(q)], CR.at[part(q)], r_cr.at[q], xp_same)
+
+    def cross_last():
+        theirs, ours = ready(LAST)
+        whole = pl.ds(0, SIZES[LAST])
+        split(CB2, whole, theirs)
+        send(CB2, CR2, r_cr2, xp_other)
+        split(CB, part(LAST), ours)
+        send(CB.at[part(LAST)], CR.at[part(LAST)], r_cr.at[LAST], xp_same)
 
     for cp in l_small:
         cp.wait()
-    l_kc.wait()
-    l_vc.wait()
 
     scale = 1.0 / HD**0.5
     slot = lax.broadcasted_iota(jnp.int32, (128, HALF), 0)
@@ -269,15 +267,14 @@
     lens = jnp.pad(CL[...], ((0, 0), (0, 112)))
 
     def attend(s):
-        if s == 0:
-            pieces = [CR[0], CR[1], CR[2, 0:16]]
-        else:
-            pieces = [CR[2, 16:32], CR[3], CR[4]]
-        got_rows = jnp.concatenate(pieces, axis=0).astype(F32)
+        mine = pl.ds(HALF * s, HALF)
+        got_rows = CR[mine, :].astype(F32)
+        if s == 1:
+            tail = CR2[...].astype(F32)
+            got_rows = got_rows + jnp.concatenate([jnp.zeros((HALF - SIZES[LAST], 4 * HD), F32), tail], axis=0)
         got_rows = jnp.concatenate(
             [got_rows[:, :HD] + got_rows[:, HD : 2 * HD], got_rows[:, 2 * HD :]], axis=1
         )
-        mine = pl.ds(HALF * s, HALF)
         qkv = (ACC[mine, :] + RO[mine, :] + got_rows).astype(BF16)
         qkv = jnp.dot(spread, qkv, preferred_element_type=F32)
         query, key_new, value_new = qkv[:, :HD], qkv[:, HD : 2 * HD], qkv[:, 2 * HD :]
@@ -313,11 +310,40 @@
         total = jnp.sum(attended * SH[...], axis=1, keepdims=True)
         return jnp.sum(jnp.where(r128 == l128, total, 0.0), axis=0, keepdims=True)
 
-    got(RO, r_so)
-    for q in range(3):
-        got(CR.at[q], r_cr.at[q])
-    reward0 = attend(0)
-
+    def spread_one(buf, slot, rsem, sem, target):
+        pltpu.make_async_remote_copy(
+            src_ref=buf.at[slot], dst_ref=buf.at[slot], send_sem=sem, recv_sem=rsem,
+            device_id=target, device_id_type=MESH,
+        ).start()
+
+    def spread_far(buf, slot, groups, rsem, sem):
+        def far(o):
+            return -(o[0] + min(o[1], 4 - o[1]) + min(o[2], 8 - o[2]))
+
+        offsets = [(i, j, k) for i in range(groups) for j in range(4) for k in range(8) if i or j or k]
+        for i, j, k in sorted(offsets, key=far):
+            spread_one(buf, slot, rsem, sem, dev((g + i) % 2, h, (y + j) % 4, (z + k) % 8, c))
+
+    pol_on(0)
+    pol_on(1)
+    pull(2)
+    pass_on(0)
+    pull(3)
+    pass_on(1)
+    pull(4)
+    pl.semaphore_wait(met3, len(near2))
+    greet(met4, planes)
+    pass_on(2)
+    pull(5)
+    exchange(0)
+    pol_pass(0)
+    pol_pass(1)
+    pass_on(3)
+    cross(0)
+    pol_pass(2)
+    exchange(1)
+    pass_on(4)
+    pass_on(5)
     got(XP.at[:, xp_rows(2 * h + 1 - c)], r_psib)
     sib_jj = y * c + (z % 4) * (1 - c)
     for k, shift in enumerate((0, 3, 1, 2)):
@@ -327,6 +353,9 @@
     for j in range(4):
         term = jnp.dot(XP[j], PW[pl.ds(SLICE * j, SLICE), :], preferred_element_type=F32)
         logits = term if logits is None else logits + term
+
+    exchange(2)
+    cross(1)
     first_col = ((g * 4 + b) * 32 + m) * VOC
     logits = logits.T
     column = lax.broadcasted_iota(jnp.int32, (VOC, 128), 0) + first_col
@@ -335,28 +364,18 @@
     stats = [peak, jnp.sum(jnp.exp(logits - peak), axis=0, keepdims=True)]
     for k in range(CAND):
         stats.append(jnp.sum(jnp.where(column == wanted[k : k + 1, :], logits, 0.0), axis=0, keepdims=True))
-    R1[b] = jnp.concatenate([*stats, jnp.zeros((4, 128), F32)], axis=0)
-    for k, other in enumerate((sib, xp_same, xp_other)):
-        send(R1.at[b], R1.at[b], r_1.at[k], other)
-
-    me = g * 32 + y * 8 + z
-
-    def spread_far(buf, rsem, sem):
-        def far(o):
-            return -(o[0] + min(o[1], 4 - o[1]) + min(o[2], 8 - o[2]))
-
-        offsets = [(i, j, k) for i in range(2) for j in range(4) for k in range(8) if i or j or k]
-        for i, j, k in sorted(offsets, key=far):
-            pltpu.make_async_remote_copy(
-                src_ref=buf.at[me], dst_ref=buf.at[me], send_sem=sem, recv_sem=rsem,
-                device_id=dev((g + i) % 2, h, (y + j) % 4, (z + k) % 8, c), device_id_type=MESH,
-            ).start()
-
-    for q in range(3, PARTS):
-        got(CR.at[q], r_cr.at[q])
-    reward1 = attend(1)
-    Q[me] = jnp.concatenate([reward0, reward1], axis=0)
-    spread_far(Q, r_q, s_q)
+    here = 2 * (2 * h + g) + c
+    R1[here] = jnp.concatenate([*stats, jnp.zeros((4, 128), F32)], axis=0)
+    for i, j, k in ((1, 0, 0), (1, 0, 1), (1, 1, 0), (1, 1, 1), (0, 1, 0), (0, 1, 1), (0, 0, 1)):
+        spread_one(R1, here, r_1, s_1, dev((g + j) % 2, (h + i) % 2, y, z, (c + k) % 2))
+
+    exchange(3)
+    cross(2)
+    exchange(4)
+    cross(3)
+    cross_last()
+    cross(4)
+    pl.semaphore_wait(met4, len(planes))
 
     sub16 = lax.broadcasted_iota(jnp.int32, (16, 128), 0)
 
@@ -368,9 +387,9 @@
             total = t * factor if total is None else total + t * factor
         return jnp.where(sub16 == 0, top, total)
 
-    for k, other in enumerate((2 * h + 1 - c, 2 * oh + c, 2 * oh + 1 - c)):
-        got(R1.at[other], r_1.at[k])
-    total = merge([R1[k] for k in range(4)])
+    got(R1.at[pl.ds(0, 7)], r_1)
+    got(R1.at[pl.ds(0, 7)], s_1)
+    total = merge([R1[k] for k in range(8)])
     mine = total
     for k in range(1, 4):
         mine = jnp.where(b == k, pltpu.roll(total, 128 - PROWS * k, 1), mine)
@@ -379,11 +398,48 @@
     for k in range(4):
         rows = jnp.concatenate([mine[4 * r + k : 4 * r + k + 1] for r in range(4)], axis=0)
         packed = jnp.where(lane4 == k, pltpu.roll(rows, PROWS * k, 1) if k else rows, packed)
-    S[me] = packed
-    spread_far(S, r_s, s_s)
+    S[y * 8 + z] = packed
+    spread_far(S, y * 8 + z, 1, r_s, s_s)
+
+    l_kc.wait()
+    l_vc.wait()
+
+    got(RO, r_so)
+    for q in range(3):
+        got(CR.at[part(q)], r_cr.at[q])
+    reward0 = attend(0)
+    for q in range(3, PARTS):
+        got(CR.at[part(q)], r_cr.at[q])
+    got(CR2, r_cr2)
+    reward1 = attend(1)
+    me = g * 32 + y * 8 + z
+    Q[me] = jnp.concatenate([reward0, reward1], axis=0)
+    spread_far(Q, me, 2, r_q, s_q)
 
     for cp in sends:
         cp.wait_send()
+    others = pl.ds(0, 31)
+    got(S.at[others], r_s)
+    first = S[:, 0, :]
+    lane1 = lax.broadcasted_iota(jnp.int32, (1, 128), 1) // PROWS
+    lane32 = lax.broadcasted_iota(jnp.int32, (32, 128), 1) // PROWS
+    top = jnp.max(first, axis=0, keepdims=True)
+    factor = pltpu.roll(jnp.exp(first - top), PROWS, 1)
+    first = jnp.sum(jnp.where(lane32 == 1, first * factor, first), axis=0, keepdims=True)
+    total = jnp.sum(S[...], axis=0)
+    total = jnp.concatenate([first, total[1:]], axis=0)
+    log_total = pltpu.roll(jnp.log(jnp.where(lane1 == 1, first, 1.0)), 128 - PROWS, 1)
+
+    def over_lanes(v):
+        v = jnp.where(lane1 == 0, v, 0.0)
+        return functools.reduce(jnp.add, [pltpu.roll(v, PROWS * k, 1) if k else v for k in range(4)])
+
+    total = total - over_lanes(top) - over_lanes(log_total)
+    for k in range(CAND):
+        r, k4 = (k + 2) // 4, (k + 2) % 4
+        row = total[r : r + 1]
+        out[k : k + 1, :] = pltpu.roll(row, 128 - PROWS * k4, 1) if k4 else row
+    got(S.at[others], s_s)
     others = pl.ds(0, 63)
     got(Q.at[others], r_q)
     reward = jnp.sum(Q[...], axis=0)
@@ -393,28 +449,6 @@
         spread_out = jnp.where(sub16 % 8 == k, pltpu.roll(both, (128 - 16 * k) % 128, 1), spread_out)
     out[16:32, :] = spread_out + jnp.pad(PV[...], ((0, 0), (0, 128 - CAND)))
     got(Q.at[others], s_q)
-
-    got(S.at[others], r_s)
-    first = S[:, 0, :]
-    lane1 = lax.broadcasted_iota(jnp.int32, (1, 128), 1) // PROWS
-    lane64 = lax.broadcasted_iota(jnp.int32, (64, 128), 1) // PROWS
-    top = jnp.max(first, axis=0, keepdims=True)
-    factor = pltpu.roll(jnp.exp(first - top), PROWS, 1)
-    first = jnp.sum(jnp.where(lane64 == 1, first * factor, first), axis=0, keepdims=True)
-    total = jnp.sum(S[...], axis=0)
-    total = jnp.concatenate([first, total[1:]], axis=0)
-    log_total = pltpu.roll(jnp.log(jnp.where(lane1 == 1, first, 1.0)), 128 - PROWS, 1)
-
-    def over_lanes(v):
-        v = jnp.where(lane1 == 0, v, 0.0)
-        return functools.reduce(jnp.add, [pltpu.roll(v, PROWS * k, 1) if k else v for k in range(4)])
-
-    total = total - over_lanes(top) - over_lanes(log_total)
-    for k in range(CAND):
-        r, k4 = (k + 2) // 4, (k + 2) % 4
-        row = total[r : r + 1]
-        out[k : k + 1, :] = pltpu.roll(row, 128 - PROWS * k4, 1) if k4 else row
-    got(S.at[others], s_s)
 
 
 def place(packed, lp_out, rw_out, x, sem):
@@ -456,15 +490,17 @@
             vm((EROWS, 3 * HD), F32),
             vm((EROWS, 3 * HD), F32),
             vm((EROWS, 3 * HD), F32),
-            vm((PARTS, PART, 3 * HD), F32),
-            vm((PARTS, PART, 3 * HD), F32),
-            vm((PARTS, PART, 3 * HD), F32),
-            vm((PARTS, PART, 4 * HD), BF16),
-            vm((PARTS, PART, 4 * HD), BF16),
-            vm((4, 16, 128), F32),
+            vm((EROWS, 3 * HD), F32),
+            vm((EROWS, 3 * HD), F32),
+            vm((EROWS, 3 * HD), F32),
+            vm((EROWS, 4 * HD), BF16),
+            vm((EROWS, 4 * HD), BF16),
+            vm((SIZES[LAST], 4 * HD), BF16),
+            vm((SIZES[LAST], 4 * HD), BF16),
+            vm((8, 16, 128), F32),
             vm((64, 2, 128), F32),
-            vm((64, 4, 128), F32),
-            dma((18,)),
+            vm((32, 4, 128), F32),
+            dma((19,)),
             dma((128,)),
             dma((2, PARTS)),
             dma,
@@ -477,11 +513,14 @@
             dma,
             dma((PARTS,)),
             dma((PARTS,)),
-            dma((3,)),
-            dma,
-            dma,
-            dma,
-            dma,
+            dma,
+            dma,
+            dma,
+            dma,
+            dma,
+            dma,
+            dma,
+            pltpu.SemaphoreType.REGULAR,
             pltpu.SemaphoreType.REGULAR,
             pltpu.SemaphoreType.REGULAR,
         ],

time: 45.6 us -> 44 us (0.965)
  Pallas kernels: 44.1 us -> 43 us
    pallas_call x1, Pallas kernels: 42.8 us -> 41.6 us  [on_device(): pl.pallas_call(kernel, out_shape=jax.ShapeDtypeStruct((32, 128), F32), in...]
where the time goes in v3:
time: 44 us; the launch traced here: 43.6 us
  Pallas kernels  43 us (98%)
  between operations  0.64 us (1%)
    pallas_call x1, Pallas kernels, on_device(): pl.pallas_call(kernel, out_shape=jax.ShapeDtypeStruct((32, 128), F32), in...  41.6 us
    pallas_call x1, Pallas kernels, on_device(): pl.pallas_call(place, out_shape=(jax.ShapeDtypeStruct((CAND, PROWS), F32)...  1.33 us

profile of v3, /device:TPU:2, one launch (start us, length us, event | category | flops | bytes accessed | tf_op | source)
XLA Modules:
  0.0 43.6 jit_solution(11868641805783564423)
XLA Ops:
  0.6 41.6 %candidates.1.packed = f32[32,128]{1,0:T(8,128)} custom-call(bf16[32,8192]{1,0:T(8,128)(2,1)} %ph.1, f32[1,8192]{1,0:T(1,128)} %bitcast.6, bf16[8192,256]{1,0:T(8,128)(2,1)} %phead.1, s32[10,128]{1,0:T(8,128)} %bitcast.8, bf16[160,8192]{1,0:T(8,128)(2,1)} %eh.1, f32[1,8192]{1,0:T(1,128)} %bitcast.7, bf16[2048,128]{1,0:T(8,128)(2,1)} %qw.1, ...), custom_call_target="tpu_custom_call" | custom-call | tf_op jit(solution)/shard_map/candidates/pallas_call | solution.py:468
  42.3 1.3 %place.1 = (f32[10,32]{1,0:T(8,128)}, f32[16,10]{1,0:T(8,128)}) custom-call(f32[32,128]{1,0:T(8,128)} %candidates.1.packed), custom_call_target="tpu_custom_call" | custom-call | tf_op jit(solution)/shard_map/place/pallas_call | solution.py:536

commit v4 on v3

--- a/solution.py
+++ b/solution.py
@@ -25,6 +25,7 @@
 SIZES = (16, 32, 32, 32, 32, 16)
 PARTS = 6
 LAST = PARTS - 1
+GROUPS = ((0, 1), (2,), (3,), (4,))
 
 
 def part(q):
@@ -35,7 +36,7 @@
     ph, pg, phead, ids, eh, eg, qw, kw, vw, kc, vc, clen, sh, prev,
     out,
     H, EG, PH, PG, PW, IDS, W, KC, VC, CL, SH, PV,
-    XR, SB, OB, XP, ACC, SO, RO, ST, RT, CS, CB, CR, CB2, CR2, R1, Q, S,
+    XR, SB, OB, XP, ACC, SO, RO, ST, RT, CS, CB, CR, CB2, CR2, R1, Q, S, SV,
     lsem, ssem, r_pull, r_sib, r_y, r_z, r_psib, r_pp, r_pn, r_pf, r_so, r_st, r_cr, r_cr2,
     r_1, s_1, r_q, s_q, r_s, s_s, met2, met3, met4,
 ):
@@ -64,6 +65,8 @@
     l_ph = load(ph, PH, 0)
     l_pg = load(pg, PG, 1)
     l_eg = load(eg, EG, 2)
+    l_h = [load(eh.at[part(q)], H.at[part(q)], 3 + q) for q in range(PARTS)]
+
     near = [sib, *opp, gydev[0], ydev[1], ydev[3], zdev[1], zdev[7]]
     near2 = [*near, ydev[2], zdev[2], zdev[6]]
     planes = [*ydev[1:], *gydev]
@@ -119,7 +122,6 @@
 
     l_ph.wait()
     l_pg.wait()
-    l_h = [load(eh.at[part(q)], H.at[part(q)], 3 + q) for q in range(PARTS)]
     lax.fori_loop(0, 2, pol_norm, 0)
     pl.semaphore_wait(barrier, len(near))
     greet(met2, near)
@@ -218,21 +220,30 @@
         send(piece, piece, r_z.at[0, q], zdev[1])
         send(piece, piece, r_z.at[1, q], zdev[7])
 
-    def ready(q):
-        for k in (1, 3, 2):
-            got(XR.at[(y - k + 4) % 4, xr_rows(2 * oh, q)], r_y.at[k - 1, q])
-        rows = xr_rows(2 * oh + 1, q)
-        got(XR.at[(z + 7) % 4, rows], r_z.at[0, q])
-        got(XR.at[(z + 1) % 4, rows], r_z.at[1, q])
-        got(XR.at[(z + 2) % 4, rows], r_z.at[2, q])
-        both = project(xr_rows(2 * oh + 1 - c, q), xr_rows(2 * oh + c, q))
-        return both[: SIZES[q]], both[SIZES[q] :]
-
-    def exchange(q):
-        theirs, ours = ready(q)
-        ST[part(q), :] = theirs
-        send(ST.at[part(q)], RT.at[part(q)], r_st.at[q], sib)
-        CS[part(q), :] = ours
+    def ready(*group):
+        for q in group:
+            for k in (1, 3, 2):
+                got(XR.at[(y - k + 4) % 4, xr_rows(2 * oh, q)], r_y.at[k - 1, q])
+            rows = xr_rows(2 * oh + 1, q)
+            got(XR.at[(z + 7) % 4, rows], r_z.at[0, q])
+            got(XR.at[(z + 1) % 4, rows], r_z.at[1, q])
+            got(XR.at[(z + 2) % 4, rows], r_z.at[2, q])
+        size = sum(SIZES[q] for q in group)
+
+        def rows_of(block):
+            return pl.ds(pl.multiple_of(EROWS * block + STARTS[group[0]], 16), size)
+
+        both = project(rows_of(2 * oh + 1 - c), rows_of(2 * oh + c))
+        return both[:size], both[size:]
+
+    def rows_in(n):
+        return pl.ds(STARTS[GROUPS[n][0]], sum(SIZES[q] for q in GROUPS[n]))
+
+    def exchange(n):
+        theirs, ours = ready(*GROUPS[n])
+        ST[rows_in(n), :] = theirs
+        send(ST.at[rows_in(n)], RT.at[rows_in(n)], r_st.at[n], sib)
+        CS[rows_in(n), :] = ours
 
     def split(ref, rows, total):
         query = total[:, :HD]
@@ -241,10 +252,10 @@
         ref[rows, HD : 2 * HD] = (query - high.astype(F32)).astype(BF16)
         ref[rows, 2 * HD :] = total[:, HD:].astype(BF16)
 
-    def cross(q):
-        got(RT.at[part(q)], r_st.at[q])
-        split(CB, part(q), CS[part(q), :] + RT[part(q), :])
-        send(CB.at[part(q)], CR.at[part(q)], r_cr.at[q], xp_same)
+    def cross(n):
+        got(RT.at[rows_in(n)], r_st.at[n])
+        split(CB, rows_in(n), CS[rows_in(n), :] + RT[rows_in(n), :])
+        send(CB.at[rows_in(n)], CR.at[rows_in(n)], r_cr.at[n], xp_same)
 
     def cross_last():
         theirs, ours = ready(LAST)
@@ -252,7 +263,7 @@
         split(CB2, whole, theirs)
         send(CB2, CR2, r_cr2, xp_other)
         split(CB, part(LAST), ours)
-        send(CB.at[part(LAST)], CR.at[part(LAST)], r_cr.at[LAST], xp_same)
+        send(CB.at[part(LAST)], CR.at[part(LAST)], r_cr.at[4], xp_same)
 
     for cp in l_small:
         cp.wait()
@@ -299,15 +310,11 @@
         whole = jnp.sum(expo, axis=1, keepdims=True) + own_expo
         weights = (expo / whole).astype(BF16)
         own_weight = (own_expo / whole).astype(BF16).astype(F32)
-        attended = jnp.concatenate(
-            [
-                jnp.dot(weights[16 * p : 16 * p + 16], VC[8 * s + p], preferred_element_type=F32)
-                for p in range(8)
-            ],
-            axis=0,
+        scored = jnp.concatenate(
+            [jnp.broadcast_to(SV[8 * s + p : 8 * s + p + 1, :], (16, CTX)) for p in range(8)], axis=0
         )
-        attended = attended + own_weight * value_new
-        total = jnp.sum(attended * SH[...], axis=1, keepdims=True)
+        total = jnp.sum(weights.astype(F32) * scored, axis=1, keepdims=True)
+        total = total + own_weight * jnp.sum(value_new * SH[...], axis=1, keepdims=True)
         return jnp.sum(jnp.where(r128 == l128, total, 0.0), axis=0, keepdims=True)
 
     def spread_one(buf, slot, rsem, sem, target):
@@ -333,15 +340,23 @@
     pull(4)
     pl.semaphore_wait(met3, len(near2))
     greet(met4, planes)
+    l_vc.wait()
+    sh0 = SH[...]
+    sh1 = sh0.astype(BF16)
+    rest = sh0 - sh1.astype(F32)
+    sh2 = rest.astype(BF16)
+    sh3 = (rest - sh2.astype(F32)).astype(BF16)
+    terms = jnp.concatenate([sh1, sh2, sh3, jnp.zeros((13, HD), BF16)], axis=0)
+    for p in range(16):
+        product = lax.dot_general(terms, VC[p], (((1,), (1,)), ((), ())), preferred_element_type=F32)
+        SV[p : p + 1, :] = product[0:1] + product[1:2] + product[2:3]
     pass_on(2)
     pull(5)
-    exchange(0)
     pol_pass(0)
     pol_pass(1)
     pass_on(3)
-    cross(0)
+    exchange(0)
     pol_pass(2)
-    exchange(1)
     pass_on(4)
     pass_on(5)
     got(XP.at[:, xp_rows(2 * h + 1 - c)], r_psib)
@@ -354,8 +369,8 @@
         term = jnp.dot(XP[j], PW[pl.ds(SLICE * j, SLICE), :], preferred_element_type=F32)
         logits = term if logits is None else logits + term
 
-    exchange(2)
-    cross(1)
+    exchange(1)
+    cross(0)
     first_col = ((g * 4 + b) * 32 + m) * VOC
     logits = logits.T
     column = lax.broadcasted_iota(jnp.int32, (VOC, 128), 0) + first_col
@@ -369,12 +384,12 @@
     for i, j, k in ((1, 0, 0), (1, 0, 1), (1, 1, 0), (1, 1, 1), (0, 1, 0), (0, 1, 1), (0, 0, 1)):
         spread_one(R1, here, r_1, s_1, dev((g + j) % 2, (h + i) % 2, y, z, (c + k) % 2))
 
+    exchange(2)
+    cross(1)
     exchange(3)
     cross(2)
-    exchange(4)
+    cross_last()
     cross(3)
-    cross_last()
-    cross(4)
     pl.semaphore_wait(met4, len(planes))
 
     sub16 = lax.broadcasted_iota(jnp.int32, (16, 128), 0)
@@ -402,14 +417,14 @@
     spread_far(S, y * 8 + z, 1, r_s, s_s)
 
     l_kc.wait()
-    l_vc.wait()
 
     got(RO, r_so)
-    for q in range(3):
-        got(CR.at[part(q)], r_cr.at[q])
+    for n in range(2):
+        got(CR.at[rows_in(n)], r_cr.at[n])
     reward0 = attend(0)
-    for q in range(3, PARTS):
-        got(CR.at[part(q)], r_cr.at[q])
+    for n in range(2, 4):
+        got(CR.at[rows_in(n)], r_cr.at[n])
+    got(CR.at[part(LAST)], r_cr.at[4])
     got(CR2, r_cr2)
     reward1 = attend(1)
     me = g * 32 + y * 8 + z
@@ -500,6 +515,7 @@
             vm((8, 16, 128), F32),
             vm((64, 2, 128), F32),
             vm((32, 4, 128), F32),
+            vm((16, CTX), F32),
             dma((19,)),
             dma((128,)),
             dma((2, PARTS)),
@@ -511,8 +527,8 @@
             dma((3, 2)),
             dma((4,)),
             dma,
-            dma((PARTS,)),
-            dma((PARTS,)),
+            dma((4,)),
+            dma((5,)),
             dma,
             dma,
             dma,

time: 44 us -> 43.3 us (0.984)
  Pallas kernels: 43 us -> 42.1 us
    pallas_call x1, Pallas kernels: 41.6 us -> 40.8 us  [on_device(): pl.pallas_call(kernel, out_shape=jax.ShapeDtypeStruct((32, 128), F32), in...]
where the time goes in v4:
time: 43.3 us; the launch traced here: 42.7 us
  Pallas kernels  42.1 us (97%)
  between operations  0.64 us (1%)
    pallas_call x1, Pallas kernels, on_device(): pl.pallas_call(kernel, out_shape=jax.ShapeDtypeStruct((32, 128), F32), in...  40.8 us
    pallas_call x1, Pallas kernels, on_device(): pl.pallas_call(place, out_shape=(jax.ShapeDtypeStruct((CAND, PROWS), F32)...  1.33 us

profile of v4, /device:TPU:2, one launch (start us, length us, event | category | flops | bytes accessed | tf_op | source)
XLA Modules:
  0.0 42.7 jit_solution(12204400217770178440)
XLA Ops:
  0.6 40.8 %candidates.1.packed = f32[32,128]{1,0:T(8,128)} custom-call(bf16[32,8192]{1,0:T(8,128)(2,1)} %ph.1, f32[1,8192]{1,0:T(1,128)} %bitcast.6, bf16[8192,256]{1,0:T(8,128)(2,1)} %phead.1, s32[10,128]{1,0:T(8,128)} %bitcast.8, bf16[160,8192]{1,0:T(8,128)(2,1)} %eh.1, f32[1,8192]{1,0:T(1,128)} %bitcast.7, bf16[2048,128]{1,0:T(8,128)(2,1)} %qw.1, ...), custom_call_target="tpu_custom_call" | custom-call | tf_op jit(solution)/shard_map/candidates/pallas_call | solution.py:483
  41.4 1.3 %place.1 = (f32[10,32]{1,0:T(8,128)}, f32[16,10]{1,0:T(8,128)}) custom-call(f32[32,128]{1,0:T(8,128)} %candidates.1.packed), custom_call_target="tpu_custom_call" | custom-call | tf_op jit(solution)/shard_map/place/pallas_call | solution.py:552

commit v5 on v4

--- a/solution.py
+++ b/solution.py
@@ -198,16 +198,14 @@
         send(piece, piece, r_pn.at[2, e], adev[2 + e])
         send(piece, piece, r_pn.at[0, e], adev[0])
         send(piece, piece, r_pn.at[1, e], adev[1])
-        if e == 1:
-            piece = XP.at[jj, xp_rows(pol_src)]
-            send(piece, piece, r_pf.at[0], sib)
+        send(piece, piece, r_pf.at[0, e], sib)
 
     def pol_pass(k):
         j = (jj + (3, 1, 2)[k]) % 4
         for e in range(2):
-            got(XP.at[j, xp_half(pol_src, e)], r_pn.at[k, e])
-        piece = XP.at[j, xp_rows(pol_src)]
-        send(piece, piece, r_pf.at[k + 1], sib)
+            piece = XP.at[j, xp_half(pol_src, e)]
+            got(piece, r_pn.at[k, e])
+            send(piece, piece, r_pf.at[k + 1, e], sib)
 
     def pass_on(q):
         piece = XR.at[y, xr_rows(2 * oh, q)]
@@ -362,7 +360,8 @@
     got(XP.at[:, xp_rows(2 * h + 1 - c)], r_psib)
     sib_jj = y * c + (z % 4) * (1 - c)
     for k, shift in enumerate((0, 3, 1, 2)):
-        got(XP.at[(sib_jj + shift) % 4, xp_rows(2 * oh + 1 - c)], r_pf.at[k])
+        for e in range(2):
+            got(XP.at[(sib_jj + shift) % 4, xp_half(2 * oh + 1 - c, e)], r_pf.at[k, e])
     l_pw.wait()
     logits = None
     for j in range(4):
@@ -525,7 +524,7 @@
             dma,
             dma((2,)),
             dma((3, 2)),
-            dma((4,)),
+            dma((4, 2)),
             dma,
             dma((4,)),
             dma((5,)),

time: 43.3 us -> 43.3 us (level)
  no operation moved by 1% of the time
where the time goes in v5:
time: 43.3 us; the launch traced here: 42.8 us
  Pallas kernels  42.2 us (97%)
  between operations  0.64 us (1%)
    pallas_call x1, Pallas kernels, on_device(): pl.pallas_call(kernel, out_shape=jax.ShapeDtypeStruct((32, 128), F32), in...  40.8 us
    pallas_call x1, Pallas kernels, on_device(): pl.pallas_call(place, out_shape=(jax.ShapeDtypeStruct((CAND, PROWS), F32)...  1.33 us

profile of v5, /device:TPU:2, one launch (start us, length us, event | category | flops | bytes accessed | tf_op | source)
XLA Modules:
  0.0 42.8 jit_solution(613313637681574282)
XLA Ops:
  0.6 40.8 %candidates.1.packed = f32[32,128]{1,0:T(8,128)} custom-call(bf16[32,8192]{1,0:T(8,128)(2,1)} %ph.1, f32[1,8192]{1,0:T(1,128)} %bitcast.6, bf16[8192,256]{1,0:T(8,128)(2,1)} %phead.1, s32[10,128]{1,0:T(8,128)} %bitcast.8, bf16[160,8192]{1,0:T(8,128)(2,1)} %eh.1, f32[1,8192]{1,0:T(1,128)} %bitcast.7, bf16[2048,128]{1,0:T(8,128)(2,1)} %qw.1, ...), custom_call_target="tpu_custom_call" | custom-call | tf_op jit(solution)/shard_map/candidates/pallas_call | solution.py:482
  41.5 1.3 %place.1 = (f32[10,32]{1,0:T(8,128)}, f32[16,10]{1,0:T(8,128)}) custom-call(f32[32,128]{1,0:T(8,128)} %candidates.1.packed), custom_call_target="tpu_custom_call" | custom-call | tf_op jit(solution)/shard_map/place/pallas_call | solution.py:551
